TPU v7x, 256 devices: a whole 4x4x8 slice. The times are simulated.
256 devices in a mesh: dp: 16 (over y, x_hi, core), tensor: 16 (over z, x_lo).
Axes of the slice: x: 4 (x_hi: 2, x_lo: 2; x = x_hi * 2 + x_lo), y: 4, z: 8, core: 2. Of those that a mesh axis runs over, the one named last changes fastest.
Arguments:
- hidden_in: bfloat16 [4096, 4096], P('dp'), may hold values from -6 to 6
- attn_gain: float32 [4096], replicated, may hold values from 0.5 to 1.5
- qkv_weight: bfloat16 [3, 4096, 4096], P(None, 'dp', 'tensor'), may hold values from -0.09375 to 0.09375
- mix_weight: bfloat16 [4096, 4096], P('tensor', 'dp'), may hold values from -0.09375 to 0.09375
- out_gain: float32 [4096], replicated, may hold values from 0.5 to 1.5
- depth_in_weight: bfloat16 [4096, 1024], P('tensor'), may hold values from -0.09375 to 0.09375
- text_table: bfloat16 [16000, 1024], P('tensor'), may hold values from -6 to 6
- code_tables: bfloat16 [7, 2048, 1024], P(None, 'tensor'), may hold values from -6 to 6
- depth_gain: float32 [1024], replicated, may hold values from 0.5 to 1.5
- depth_qkv: bfloat16 [3, 1024, 1024], P(None, 'dp'), may hold values from -0.1875 to 0.1875
- depth_mix: bfloat16 [1024, 1024], replicated, may hold values from -0.1875 to 0.1875
- final_gain: float32 [1024], replicated, may hold values from 0.5 to 1.5
- heads_weight: bfloat16 [8, 1024, 2048], P(None, None, 'tensor'), may hold values from -0.59765625 to 0.59765625
- text_ids: int32 [4096], P('dp'), may hold values from 0 to 15999
- codes: int32 [4096, 8], P('dp'), may hold values from 0 to 2047
Outputs:
- token_loss: float32 [4096, 8], P(('dp', 'tensor'))
All inputs are finite; a program needn't handle non-finite values.
Results may differ from a plain program's by a relative error of at most 0.005.
Values may be sent and summed in bfloat16 or wider, within the bound.
A program may use at most 128 MiB of HBM per device.

v0:
```python
import math

import jax
import jax.numpy as jnp
from jax import lax
from jax.sharding import PartitionSpec as P

D = 4096
HEAD_DIM = 128
FRAMES = 256
DD = 1024
DHEADS = 16
DHEAD_DIM = 64
CODEBOOKS = 8


epsilon = 1e-05


def rms_factor(values):
    return lax.rsqrt(jnp.mean(values * values, axis=-1, keepdims=True) + epsilon)


def rotate_halves(tensor, positions):
    half_dim = tensor.shape[-1] // 2
    frequency = jnp.exp(jnp.arange(half_dim, dtype=jnp.float32) * (-math.log(10000.0) / half_dim))
    angles = positions[:, None] * frequency[None, :]
    cosine = jnp.cos(angles)[:, None, :]
    sine_part = jnp.sin(angles)[:, None, :]
    first_half = tensor[..., :half_dim]
    second_half = tensor[..., half_dim:]
    return jnp.concatenate(
        [
            first_half * cosine - second_half * sine_part,
            second_half * cosine + first_half * sine_part,
        ],
        axis=-1,
    )


def temporal_mix(normed, qkv_cols):
    row_count = normed.shape[0]
    col_width = qkv_cols.shape[2]
    seq_count = row_count // FRAMES
    head_count = col_width // HEAD_DIM
    projected = jnp.einsum("rd,idw->irw", normed, qkv_cols, preferred_element_type=jnp.float32)
    projected = projected.reshape(3, seq_count, FRAMES, head_count, HEAD_DIM)
    positions = jnp.arange(FRAMES, dtype=jnp.float32)
    queries = rotate_halves(projected[0], positions).astype(jnp.bfloat16)
    keys_rot = rotate_halves(projected[1], positions).astype(jnp.bfloat16)
    values_all = projected[2].astype(jnp.bfloat16)
    scores = jnp.einsum(
        "sqhd,skhd->shqk", queries, keys_rot, preferred_element_type=jnp.float32
    ) * HEAD_DIM ** (-0.5)
    order = jnp.arange(FRAMES)
    causal = order[:, None] >= order[None, :]
    exp_scores = jnp.where(causal, jnp.exp(jnp.where(causal, scores, 0.0)), 0.0)
    weights = (exp_scores / jnp.sum(exp_scores, axis=-1, keepdims=True)).astype(jnp.bfloat16)
    attended = jnp.einsum(
        "shqk,skhd->sqhd", weights, values_all, preferred_element_type=jnp.float32
    )
    return attended.astype(jnp.bfloat16).reshape(row_count, col_width)


def depth_mixer(projected, mix_weight):
    row_count = projected.shape[1]
    split = projected.reshape(3, row_count, CODEBOOKS, DHEADS, DHEAD_DIM)
    scores = jnp.einsum(
        "rqhd,rkhd->rhqk", split[0], split[1], preferred_element_type=jnp.float32
    ) * DHEAD_DIM ** (-0.5)
    order = jnp.arange(CODEBOOKS)
    causal = order[:, None] >= order[None, :]
    exp_scores = jnp.where(causal, jnp.exp(jnp.where(causal, scores, 0.0)), 0.0)
    weights = (exp_scores / jnp.sum(exp_scores, axis=-1, keepdims=True)).astype(jnp.bfloat16)
    attended = jnp.einsum("rhqk,rkhd->rqhd", weights, split[2], preferred_element_type=jnp.float32)
    attended = attended.astype(jnp.bfloat16).reshape(row_count, CODEBOOKS, DD)
    return jnp.einsum("rcd,de->rce", attended, mix_weight, preferred_element_type=jnp.float32)


def local_embeds(text_table, code_tables, text_ids, codes, rank_tensor):
    text_count = text_table.shape[0]
    text_local = text_ids - rank_tensor * text_count
    text_owned = (text_local >= 0) & (text_local < text_count)
    text_found = jnp.take(text_table, jnp.clip(text_local, 0, text_count - 1), axis=0)
    text_part = jnp.where(text_owned[:, None], text_found.astype(jnp.float32), 0.0)
    code_count = code_tables.shape[1]
    code_local = codes[:, : CODEBOOKS - 1] - rank_tensor * code_count
    code_owned = (code_local >= 0) & (code_local < code_count)
    books = jnp.arange(CODEBOOKS - 1, dtype=jnp.int32)[None, :]
    code_found = code_tables[books, jnp.clip(code_local, 0, code_count - 1)]
    code_part = jnp.where(code_owned[:, :, None], code_found.astype(jnp.float32), 0.0)
    return jnp.concatenate([text_part[:, None, :], code_part], axis=1)


def arrive_embeds(embeds):
    return lax.psum_scatter(
        embeds.astype(jnp.bfloat16), "tensor", scatter_dimension=0, tiled=True
    ).astype(jnp.float32)


def shards(
    hidden_in,
    attn_gain,
    qkv_weight,
    mix_weight,
    out_gain,
    depth_in_weight,
    text_table,
    code_tables,
    depth_gain,
    depth_qkv,
    depth_mix,
    final_gain,
    heads_weight,
    text_ids,
    codes,
):
    rank_tensor = lax.axis_index("tensor")
    group_size = lax.axis_size("tensor")
    local_rows = hidden_in.shape[0]
    own_rows = local_rows // group_size
    own_start = rank_tensor * own_rows
    qkv_full, mix_full, depth_full = (
        lax.all_gather(qkv_weight, "dp", axis=1, tiled=True),
        lax.all_gather(mix_weight, "dp", axis=1, tiled=True),
        lax.all_gather(depth_qkv, "dp", axis=1, tiled=True),
    )
    hidden_f = hidden_in.astype(jnp.float32)
    normed = (hidden_f * rms_factor(hidden_f) * attn_gain).astype(jnp.bfloat16)
    attended = temporal_mix(normed, qkv_full)
    partial_mix = jnp.dot(attended, mix_full, preferred_element_type=jnp.float32)
    embeds = local_embeds(text_table, code_tables, text_ids, codes, rank_tensor)
    embed_rows = arrive_embeds(embeds)
    feat_width = depth_in_weight.shape[0]
    feat_start = rank_tensor * feat_width
    summed_cols = lax.psum_scatter(
        partial_mix.astype(jnp.bfloat16), "tensor", scatter_dimension=1, tiled=True
    ).astype(jnp.float32)
    resid_cols = summed_cols + lax.dynamic_slice_in_dim(hidden_f, feat_start, feat_width, 1)
    square_part = jnp.sum(resid_cols * resid_cols, axis=1)
    gain_cols = lax.dynamic_slice_in_dim(out_gain, feat_start, feat_width, 0)
    scaled_cols = (resid_cols * gain_cols).astype(jnp.bfloat16)
    context_part = jnp.dot(scaled_cols, depth_in_weight, preferred_element_type=jnp.float32)
    context_sum, square_sum = (
        lax.psum_scatter(
            context_part.astype(jnp.bfloat16), "tensor", scatter_dimension=0, tiled=True
        ).astype(jnp.float32),
        lax.psum_scatter(
            square_part.astype(jnp.bfloat16), "tensor", scatter_dimension=0, tiled=True
        ).astype(jnp.float32),
    )
    context = context_sum * lax.rsqrt(square_sum / D + epsilon)[:, None]
    depth_input = context[:, None, :] + embed_rows
    dnormed = (depth_input * rms_factor(depth_input) * depth_gain).astype(jnp.bfloat16)
    projected = jnp.einsum("rcd,ide->irce", dnormed, depth_full, preferred_element_type=jnp.float32)
    depth_out = depth_input + depth_mixer(projected.astype(jnp.bfloat16), depth_mix)
    final = (depth_out * rms_factor(depth_out) * final_gain).astype(jnp.bfloat16)
    final_all = lax.all_gather(final, "tensor", axis=0, tiled=True)
    logits = jnp.einsum("rcd,cdv->rcv", final_all, heads_weight, preferred_element_type=jnp.float32)
    vocab_width = heads_weight.shape[2]
    target_local = codes - rank_tensor * vocab_width
    matches = jnp.arange(vocab_width, dtype=jnp.int32)[None, None, :] == target_local[:, :, None]
    target_part = jnp.sum(jnp.where(matches, logits, 0.0), axis=-1)
    exp_part = jnp.sum(jnp.exp(logits), axis=-1)
    exp_total, target_total = lax.psum((exp_part, target_part), "tensor")
    losses = jnp.log(exp_total) - target_total
    return lax.dynamic_slice_in_dim(losses, own_start, own_rows, 0)


def solution(mesh):
    in_specs = (
        P("dp", None),
        P(),
        P(None, "dp", "tensor"),
        P("tensor", "dp"),
        P(),
        P("tensor", None),
        P("tensor", None),
        P(None, "tensor", None),
        P(),
        P(None, "dp", None),
        P(),
        P(),
        P(None, None, "tensor"),
        P("dp"),
        P("dp", None),
    )
    out_specs = P(("dp", "tensor"), None)
    return jax.shard_map(shards, mesh=mesh, in_specs=in_specs, out_specs=out_specs, check_vma=False)
```

profile of v0, /device:TPU:4, one launch (start us, length us, event | category | flops | bytes accessed | tf_op | source)
XLA Modules:
  0.0 645.7 jit_solution(13716090094720428637)
XLA Ops:
  6.5 2.1 copy.45
  12.7 69.6 %all-gather.5.cloned.1.call-done = bf16[3,4096,256]{1,2,0:T(8,128)(2,1)} async-done(((bf16[3,256,256]{1,2,0:T(8,128)(2,1)}), bf16[3,4096,256]{1,2,0:T(8,128)(2,1)}) %all-gather.5.cloned.1.call-update) | async-done | bytes 6291472 | tf_op jit(solution)/shard_map/all_gather | solution.py:124
  82.3 5.3 fusion.24
  91.4 43.3 %all-gather.7.cloned.1.call-done = bf16[256,4096]{1,0:T(8,128)(2,1)} async-done(((bf16[256,256]{1,0:T(8,128)(2,1)}), bf16[256,4096]{1,0:T(8,128)(2,1)}) %all-gather.7.cloned.1.call-update) | async-done | bytes 2097168 | tf_op jit(solution)/shard_map/all_gather | solution.py:125
  134.7 3.6 convolution_convert_fusion
  138.5 4.1 convert_element_type.93
  142.9 34.8 %gather_fusion.1 = bf16[1792,1024]{1,0:T(8,128)(2,1)} fusion(bf16[7,128,1024]{2,1,0:T(8,128)(2,1)} %param.22, s32[1792]{0:T(1024)S(1)} %reshape.218), kind=kCustom, calls=%fused_computation.1 | custom fusion | bytes 7354368 | tf_op jit(solution)/shard_map/gather | solution.py:90
  177.7 6.5 reshape.225
  185.2 3.4 gather_fusion
  188.6 24.9 %reduce-scatter.4.cloned.1.call-done = bf16[256,256]{1,0:T(8,128)(2,1)} async-done(((bf16[256,4096]{1,0:T(8,128)(2,1)}), bf16[256,256]{1,0:T(8,128)(2,1)}) %reduce-scatter.4.cloned.1.call-update) | async-done | bytes 131088 | tf_op jit(solution)/shard_map/reduce_scatter | solution.py:136
  213.5 2.1 convolution_convert_fusion.2
  215.8 2.7 select_convert_fusion
  218.5 3.1 fusion.35
  221.7 3.5 pad_maximum_fusion
  228.2 32.4 %all-reduce = bf16[256]{0:T(256)(128)(2,1)S(1)} all-reduce(bf16[256]{0:T(256)(128)(2,1)S(1)} %multiply_reduce_fusion.3), channel_id=4, replica_groups=mesh['dp'=16,'tensor'=16] {'tensor'}, use_global_device_ids=true, to_apply=%region_5.6.clone | all-reduce | flops 256 | bytes 1024
  260.6 24.9 %reduce-scatter.6.cloned.1.call-done = bf16[16,1024]{1,0:T(8,128)(2,1)} async-done(((bf16[256,1024]{1,0:T(8,128)(2,1)}), bf16[16,1024]{1,0:T(8,128)(2,1)}) %reduce-scatter.6.cloned.1.call-update) | async-done | bytes 32784 | tf_op jit(solution)/shard_map/reduce_scatter | solution.py:145
  286.3 100.3 %reduce-scatter.8.cloned.1.call-done = bf16[16,8,1024]{2,1,0:T(8,128)(2,1)} async-done(((bf16[256,8,1024]{2,1,0:T(8,128)(2,1)}), bf16[16,8,1024]{2,1,0:T(8,128)(2,1)}) %reduce-scatter.8.cloned.1.call-update) | async-done | bytes 262160 | tf_op jit(solution)/shard_map/reduce_scatter | solution.py:96
  387.7 68.6 %all-gather.9.cloned.1.call-done = bf16[3,1024,1024]{2,1,0:T(8,128)(2,1)} async-done(((bf16[3,64,1024]{2,1,0:T(8,128)(2,1)}), bf16[3,1024,1024]{2,1,0:T(8,128)(2,1)}) %all-gather.9.cloned.1.call-update) | async-done | bytes 6291472 | tf_op jit(solution)/shard_map/all_gather | solution.py:126
  456.3 3.9 fusion.21
  462.9 2.5 fusion.20
  465.4 3.2 fusion.30
  471.5 99.0 %all-gather.11.cloned.1.call-done = bf16[256,8,1024]{2,1,0:T(8,128)(2,1)} async-done(((bf16[16,8,1024]{2,1,0:T(8,128)(2,1)}), bf16[256,8,1024]{2,1,0:T(8,128)(2,1)}) %all-gather.11.cloned.1.call-update) | async-done | bytes 4194320 | tf_op jit(solution)/shard_map/all_gather | solution.py:158
  570.5 5.6 exponential_reduce_fusion
  576.1 62.1 %all-reduce.1 = (f32[256,8]{0,1:T(8,128)S(1)}, f32[256,8]{0,1:T(8,128)S(1)}) all-reduce(f32[256,8]{0,1:T(8,128)S(1)} %get-tuple-element.6, f32[256,8]{0,1:T(8,128)S(1)} %get-tuple-element.5), channel_id=1, replica_groups=mesh['dp'=16,'tensor'=16] {'tensor'}, use_global_device_ids=true, to_apply=%region_13.14 | all-reduce | flops 4096 | bytes 32768 | tf_op jit(solution)/shard_map/psum | solution.py:165
  (74 shorter events, 20.0 us)
Async XLA Ops:
  6.5 463.5 %copy-start = (bf16[1024,1024]{1,0:T(8,128)(2,1)S(1)}, bf16[1024,1024]{1,0:T(8,128)(2,1)}, u32[]{:S(2)}) copy-start(bf16[1024,1024]{1,0:T(8,128)(2,1)} %param.25) | copy-start | bytes 6291460
  6.5 75.8 %all-gather.5.cloned.1.call-start = ((), (), s32[]{:S(2)}) async-start(), calls=%async_computation.3 | async-start | bytes 6684672 | tf_op jit(solution)/shard_map/all_gather | solution.py:124
  8.7 126.1 %all-gather.7.cloned.1.call-start = ((), (), s32[]{:S(2)}) async-start(), calls=%async_computation.4 | async-start | bytes 2228224 | tf_op jit(solution)/shard_map/all_gather | solution.py:125
  9.4 204.0 %reduce-scatter.4.cloned.1.call-start = ((), (), s32[]{:S(2)}) async-start(), calls=%async_computation.5 | async-start | bytes 2228224 | tf_op jit(solution)/shard_map/reduce_scatter | solution.py:136
  138.4 4.2 copy-start.4
  138.4 147.1 %reduce-scatter.6.cloned.1.call-start = ((), (), s32[]{:S(2)}) async-start(), calls=%async_computation.6 | async-start | bytes 557056 | tf_op jit(solution)/shard_map/reduce_scatter | solution.py:145
  177.7 7.4 %copy-start.6 = (s32[256]{0:T(256)S(1)}, s32[256]{0:T(256)}, u32[]{:S(2)}) copy-start(s32[256]{0:T(256)} %param.28) | copy-start | bytes 3076
  184.2 29.3 %copy-start.2 = (bf16[256,1024]{1,0:T(8,128)(2,1)S(1)}, bf16[256,1024]{1,0:T(8,128)(2,1)}, u32[]{:S(2)}) copy-start(bf16[256,1024]{1,0:T(8,128)(2,1)} %param.20) | copy-start | bytes 1572868
  215.6 171.0 %reduce-scatter.8.cloned.1.call-start = ((), (), s32[]{:S(2)}) async-start(), calls=%async_computation.7 | async-start | bytes 4456448 | tf_op jit(solution)/shard_map/reduce_scatter | solution.py:96
  225.1 0.7 copy-start.8
  225.1 1.9 copy-start.3
  225.1 231.2 %copy-start.7 = (f32[1024]{0:T(1024)S(1)}, f32[1024]{0:T(1024)}, u32[]{:S(2)}) copy-start(f32[1024]{0:T(1024)} %param.23) | copy-start | bytes 12292
  225.2 231.1 %all-gather.9.cloned.1.call-start = ((), (), s32[]{:S(2)}) async-start(), calls=%async_computation.8 | async-start | bytes 6684672 | tf_op jit(solution)/shard_map/all_gather | solution.py:126
  225.7 344.7 %all-gather.11.cloned.1.call-start = ((), (), s32[]{:S(2)}) async-start(), calls=%async_computation.9 | async-start | bytes 4456448 | tf_op jit(solution)/shard_map/all_gather | solution.py:158
  465.4 4.7 copy-start.1
  465.4 5.3 copy-start.5
Sparse Core Ops, SparseCore 0:
  10.0 72.2 all-gather.4
  84.9 49.7 all-gather.6
  138.5 74.8 reduce-scatter.3
  215.8 69.6 reduce-scatter.5
  288.1 98.5 reduce-scatter.7
  389.6 66.6 all-gather.8
  471.6 98.8 all-gather.10
where the time goes:
time: 647 us; the launch traced here: 646 us
  waiting for transfers between devices  432 us (67%)
  blocking collectives  94.5 us (15%)
  local copies, waits for them, and re-layouts  54.1 us (8%)
  matrix products  29.1 us (4%)
  other arithmetic  21.4 us (3%)
  between operations  14.4 us (2%)
    reduce_scatter x1, waiting for transfers between devices, arrive_embeds(): lax.psum_scatter(embeds.astype(jnp.bfloat16), 'tensor', scatter_dimension...  100 us
    all_gather x1, waiting for transfers between devices, shards(): final_all = lax.all_gather(final, 'tensor', axis=0, tiled=True)  99 us
    all_gather x1, waiting for transfers between devices, shards(): lax.all_gather(qkv_weight, 'dp', axis=1, tiled=True)  69.6 us
    all_gather x1, waiting for transfers between devices, shards(): lax.all_gather(depth_qkv, 'dp', axis=1, tiled=True)  68.6 us
    psum x1, blocking collectives, shards(): exp_total, target_total = lax.psum((exp_part, target_part), 'tensor')  62.1 us
    all_gather x1, waiting for transfers between devices, shards(): lax.all_gather(mix_weight, 'dp', axis=1, tiled=True)  43.3 us
    gather x1, local copies, waits for them, and re-layouts, local_embeds(): code_found = code_tables[books, jnp.clip(code_local, 0, code_count - 1)]  34.8 us
    unnamed x1, blocking collectives  32.4 us
  transfers between devices with their start and end apart: 7, of which 7 were waited for; matrix products, arithmetic and copies ran while one was open for 12% of the time, Pallas kernels for 0%

commit v1 on v0

v1 whole, which is shorter than its diff:
```python
import functools

import jax
import jax.numpy as jnp
import numpy as np
from jax import lax
from jax.experimental import pallas as pl
from jax.experimental.pallas import tpu as pltpu
from jax.sharding import PartitionSpec as P

D = 4096
HEAD_DIM = 128
FRAMES = 256
DD = 1024
DHEADS = 16
DHEAD_DIM = 64
CODEBOOKS = 8
DP = 16
TP = 16
NZ = 8
OWN = 16
F32 = jnp.float32
BF16 = jnp.bfloat16
MESH = pl.DeviceIdType.MESH

epsilon = 1e-05

X0, R1, L1, R2, L2, R3, L3, C0 = range(8)


def dot(a, b):
    return jnp.dot(a, b, preferred_element_type=F32)


def dot_t(a, b):
    return lax.dot_general(a, b, (((1,), (1,)), ((), ())), preferred_element_type=F32)


class Places:
    def __init__(self):
        d = lax.axis_index("dp")
        t = lax.axis_index("tensor")
        self.d, self.t = d, t
        self.core = lax.rem(d, 2)
        self.xh = lax.rem(d // 2, 2)
        self.xl = lax.rem(t, 2)
        self.z = t // 2
        self.up = lax.rem(d + 4, 16)
        self.down = lax.rem(d + 12, 16)
        self.far = lax.rem(d + 8, 16)
        self.xstep = 2 - 4 * self.xh
        self.xpeer = d + self.xstep
        self.cstep = 1 - 2 * self.core
        self.cpeer = d + self.cstep
        self.xsib = t + 1 - 2 * self.xl
        self.zup = lax.rem(t + 2, 16)
        self.zdown = lax.rem(t + 14, 16)
        self.blocks = [d, self.xpeer, self.down, self.up, self.down + self.xstep,
                       self.up + self.xstep, self.far, self.far + self.xstep]


class Flow:
    def __init__(self, pos, own, block, send_sem, recv_sem):
        self.pos, self.own, self.block = pos, own, block
        self.ss, self.rs = send_sem, recv_sem

    def copy(self, kind, idx, dev, own=False):
        src = self.own if own else self.block(idx)
        return pltpu.make_async_remote_copy(
            src_ref=src, dst_ref=self.block(idx), send_sem=self.ss(kind), recv_sem=self.rs(kind),
            device_id={"dp": dev}, device_id_type=MESH)

    def start0(self):
        p = self.pos
        for kind, dev in ((X0, p.xpeer), (R1, p.up), (L1, p.down), (C0, p.cpeer)):
            self.copy(kind, p.d, dev, own=True).start()

    def got(self, kind):
        p = self.pos
        self.copy(kind, p.blocks[kind + 1], p.cpeer).wait_recv()

    def forward(self, kind, idx, dev):
        self.copy(kind, idx, dev).start()

    def to_core(self, kind):
        p = self.pos
        self.forward(C0 + kind + 1, p.blocks[kind + 1], p.cpeer)

    def stage1(self):
        p = self.pos
        self.got(X0)
        self.forward(R2, p.xpeer, p.up)
        self.forward(L2, p.xpeer, p.down)
        self.to_core(X0)
        self.got(R1)
        self.forward(R3, p.down, p.up)
        self.to_core(R1)
        self.got(L1)
        self.to_core(L1)

    def stage2(self):
        p = self.pos
        self.got(R2)
        self.to_core(R2)
        self.got(L2)
        self.forward(L3, p.up + p.xstep, p.down)
        self.to_core(L2)

    def stage3(self):
        self.got(R3)
        self.to_core(R3)
        self.got(L3)
        self.to_core(L3)

    def stage4(self):
        p = self.pos
        for n in range(8):
            self.copy(C0 + n, p.blocks[n] + p.cstep, p.cpeer).wait_recv()

    def drain(self):
        p = self.pos
        for kind in range(15):
            self.copy(kind, p.d, p.cpeer).wait_send()


class Ring:
    def __init__(self, pos, own, right, left, out, inn, ss, rs, base):
        self.pos, self.own = pos, own
        self.right, self.left, self.out, self.inn = right, left, out, inn
        self.ss, self.rs, self.base = ss, rs, base

    def dest(self, right, s):
        z = self.pos.z
        return lax.rem(z + 4 - s, NZ) if right else lax.rem(z + 5 + s, NZ)

    def copy(self, right, s):
        slots = self.right if right else self.left
        k = self.base + s + (0 if right else 4)
        src = self.own(self.dest(right, s)) if s == 0 else slots.at[s - 1]
        return pltpu.make_async_remote_copy(
            src_ref=src, dst_ref=slots.at[s], send_sem=self.ss.at[k], recv_sem=self.rs.at[k],
            device_id={"tensor": self.pos.zup if right else self.pos.zdown}, device_id_type=MESH)

    def step(self, s):
        for right in (True, False):
            if s > (3 if right else 2):
                continue
            if s:
                self.copy(right, s - 1).wait_recv()
                slots = self.right if right else self.left
                mine = self.own(self.dest(right, s))
                for h in range(2):
                    slots[s - 1, h] = (slots[s - 1, h].astype(F32) + mine[h].astype(F32)).astype(BF16)
            self.copy(right, s).start()

    def total(self, h):
        mine = self.own(self.pos.z)
        return mine[h].astype(F32) + self.right[3, h].astype(F32) + self.left[2, h].astype(F32)

    def pair(self):
        return pltpu.make_async_remote_copy(
            src_ref=self.out, dst_ref=self.inn, send_sem=self.ss.at[self.base + 7],
            recv_sem=self.rs.at[self.base + 7], device_id={"tensor": self.pos.xsib}, device_id_type=MESH)

    def finish(self):
        self.copy(True, 3).wait_recv()
        self.copy(False, 2).wait_recv()
        self.out[...] = self.total(1 - self.pos.xl).astype(BF16)
        self.pair().start()

    def result(self):
        self.pair().wait_recv()
        return self.total(self.pos.xl) + self.inn[...].astype(F32)

    def drain(self):
        for s in range(4):
            self.copy(True, s).wait_send()
        for s in range(3):
            self.copy(False, s).wait_send()
        self.pair().wait_send()


def front(hid, gain, qkv, mix, ogain, din, text, tabs, tid, code, cosr, sinr, dqkv, heads,
          depth_in, dfull, hfull,
          wall, normed, acc, att, part, emb, er, el, eo, ei, pr, pl_, po, pi, ctxs, ctxr, sqs, sqr,
          wss, wrs, ess, ers, pss, prs, css, crs, hss, hrs, lsem):
    p = Places()
    d, t = p.d, p.t

    barrier = pltpu.get_barrier_semaphore()
    for dev in (p.xpeer, p.up, p.down, p.cpeer):
        pl.semaphore_signal(barrier, inc=1, device_id={"dp": dev}, device_id_type=MESH)
    for k in range(1, TP):
        pl.semaphore_signal(barrier, inc=1, device_id={"tensor": lax.rem(t + k, TP)}, device_id_type=MESH)
    pl.semaphore_wait(barrier, 4 + TP - 1)

    def flow(f):
        own = mix if f == 3 else qkv.at[f]
        return Flow(p, own, lambda i: wall.at[f, i], lambda k: wss.at[f, k], lambda k: wrs.at[f, k])

    flows = [flow(f) for f in range(4)]
    deep = Flow(p, dqkv, lambda i: dfull.at[:, pl.ds(pl.multiple_of(i * 64, 64), 64), :],
                lambda k: wss.at[4, k], lambda k: wrs.at[4, k])
    for f in flows:
        f.start0()
    own_deep = pltpu.make_async_copy(dqkv, dfull.at[:, pl.ds(pl.multiple_of(d * 64, 64), 64), :], lsem.at[0])
    own_heads = pltpu.make_async_copy(heads, hfull.at[p.xl], lsem.at[1])
    own_deep.start()
    own_heads.start()

    lanes = lax.broadcasted_iota(jnp.int32, (FRAMES, 128), 1)

    def place(c, found):
        emb[:, c] = found.astype(BF16).reshape(TP, OWN, DD)

    rows = text.shape[0]
    wide = lax.broadcasted_iota(jnp.int32, (FRAMES, rows), 1)
    place(0, dot((wide == tid[...]).astype(BF16), text[...]))
    for c in range(1, CODEBOOKS):
        place(c, dot((lanes == code[:, c - 1:c]).astype(BF16), tabs[c - 1]))
    eown = lambda z: emb.at[pl.ds(2 * z, 2)]
    ering = Ring(p, eown, er, el, eo, ei, ess, ers, 0)
    ering.step(0)

    for f in range(3):
        wall[f, d] = qkv[f]
    wall[3, d] = mix[...]

    def norm_rows(n, carry):
        r = pl.ds(pl.multiple_of(n * 32, 32), 32)
        h = hid[r, :].astype(F32)
        scale = lax.rsqrt(jnp.mean(h * h, axis=-1, keepdims=True) + epsilon)
        normed[r, :] = (h * scale * gain[...]).astype(BF16)
        return carry

    lax.fori_loop(0, FRAMES // 32, norm_rows, 0)

    for f in flows:
        f.stage1()
    for f in flows:
        f.stage2()
    ering.step(1)
    for f in flows:
        f.stage3()
    for f in flows[:3]:
        f.stage4()
    deep.start0()
    head_part = pl.ds(p.core * 4, 4)
    head_rest = pl.ds(4 - p.core * 4, 4)
    head_x = pltpu.make_async_remote_copy(
        src_ref=heads.at[head_part], dst_ref=hfull.at[p.xl, head_part], send_sem=hss.at[0],
        recv_sem=hrs.at[0], device_id={"tensor": p.xsib}, device_id_type=MESH)
    head_x.start()
    ering.step(2)

    acc[...] = jnp.zeros_like(acc)

    def project(b, carry):
        cols = normed[:, pl.ds(pl.multiple_of(b * 256, 256), 256)]
        for i in range(3):
            acc[i] += dot(cols, wall[i, b])
        return carry

    lax.fori_loop(0, DP, project, 0)

    order_q = lax.broadcasted_iota(jnp.int32, (FRAMES, FRAMES), 0)
    order_k = lax.broadcasted_iota(jnp.int32, (FRAMES, FRAMES), 1)
    causal = order_q >= order_k
    cosv, sinv = cosr[...], sinr[...]

    def rotate(v):
        half = HEAD_DIM // 2
        swapped = jnp.concatenate([v[:, half:], v[:, :half]], axis=1)
        return (v * cosv + swapped * sinv).astype(BF16)

    for h in range(2):
        cols = slice(h * HEAD_DIM, (h + 1) * HEAD_DIM)
        q = rotate(acc[0, :, cols])
        k = rotate(acc[1, :, cols])
        v = acc[2, :, cols].astype(BF16)
        scores = dot_t(q, k) * HEAD_DIM ** (-0.5)
        e = jnp.where(causal, jnp.exp(jnp.where(causal, scores, 0.0)), 0.0)
        w = (e / jnp.sum(e, axis=-1, keepdims=True)).astype(BF16)
        att[:, cols] = dot(w, v).astype(BF16)

    flows[3].stage4()
    ering.step(3)
    pown = lambda z: part.at[pl.ds(2 * z, 2)]
    pring = Ring(p, pown, pr, pl_, po, pi, pss, prs, 0)

    def mixed(offset):
        z = lax.rem(p.z + offset, NZ)
        for h in range(2):
            part[2 * z + h] = dot(att[...], wall[3, 2 * z + h]).astype(BF16)

    mixed(4)
    mixed(5)
    pring.step(0)
    mixed(3)
    mixed(6)
    deep.stage1()
    pring.step(1)
    mixed(2)
    mixed(7)
    deep.stage2()
    pring.step(2)
    mixed(1)
    mixed(0)
    deep.stage3()
    pring.step(3)
    head_x_in = pltpu.make_async_remote_copy(
        src_ref=hfull.at[1 - p.xl, head_part], dst_ref=hfull.at[1 - p.xl, head_part], send_sem=hss.at[1],
        recv_sem=hrs.at[0], device_id={"dp": p.cpeer}, device_id_type=MESH)
    head_x_in.wait_recv()
    head_c = pltpu.make_async_remote_copy(
        src_ref=hfull.at[1 - p.xl, head_part], dst_ref=hfull.at[1 - p.xl, head_part], send_sem=hss.at[1],
        recv_sem=hrs.at[1], device_id={"dp": p.cpeer}, device_id_type=MESH)
    head_c.start()
    pring.finish()
    ering.finish()

    cols = pl.ds(pl.multiple_of(t * 256, 256), 256)
    resid = pring.result() + hid[:, cols].astype(F32)
    square = jnp.sum(resid * resid, axis=-1, keepdims=True)
    sqs[...] = jnp.broadcast_to(square, (FRAMES, 128)).reshape(TP, OWN, 128)
    scaled = (resid * ogain[:, cols]).astype(BF16)
    ctxs[...] = dot(scaled, din[...]).astype(BF16).reshape(TP, OWN, DD)

    def share(k, which, sender):
        src, dst = (ctxs, ctxr) if which == 0 else (sqs, sqr)
        to = lax.rem(t + k, TP)
        return pltpu.make_async_remote_copy(
            src_ref=src.at[to], dst_ref=dst.at[sender], send_sem=css.at[which, k], recv_sem=crs.at[which, k],
            device_id={"tensor": to}, device_id_type=MESH)

    for k in range(1, TP):
        for which in range(2):
            share(k, which, t).start()
    ctxr[t] = ctxs[t]
    sqr[t] = sqs[t]
    embeds = ering.result().reshape(CODEBOOKS, OWN, DD)
    for k in range(1, TP):
        for which in range(2):
            share(k, which, lax.rem(t + TP - k, TP)).wait_recv()
    context = ctxr[0].astype(F32)
    squares = sqr[0]
    for n in range(1, TP):
        context = context + ctxr[n].astype(F32)
        squares = squares + sqr[n]
    context = context * lax.rsqrt(squares[:, :1] / D + epsilon)
    depth_in[...] = context[None] + embeds

    deep.stage4()
    head_rest_in = pltpu.make_async_remote_copy(
        src_ref=hfull.at[1 - p.xl, head_rest], dst_ref=hfull.at[1 - p.xl, head_rest], send_sem=hss.at[1],
        recv_sem=hrs.at[1], device_id={"dp": p.cpeer}, device_id_type=MESH)
    head_rest_in.wait_recv()
    own_deep.wait()
    own_heads.wait()
    for f in flows:
        f.drain()
    deep.drain()
    ering.drain()
    pring.drain()
    for k in range(1, TP):
        for which in range(2):
            share(k, which, t).wait_send()
    head_x.wait_send()
    head_c.wait_send()


def back(depth_in, dfull, dgain, dmix, fgain, hfull, target,
         loss,
         wq, wm, wh, proj, att, fin, sums, got, lsem, ss, rs, tss, trs):
    t = lax.axis_index("tensor")
    z = t // 2
    xl = lax.rem(t, 2)
    zup, zdown = lax.rem(t + 2, 16), lax.rem(t + 14, 16)

    loads = [pltpu.make_async_copy(dfull.at[i], wq.at[i], lsem.at[i]) for i in range(3)]
    loads.append(pltpu.make_async_copy(dmix, wm, lsem.at[3]))
    for h in range(2):
        loads.append(pltpu.make_async_copy(hfull.at[h], wh.at[:, :, pl.ds(h * 128, 128)], lsem.at[4 + h]))
    for one in loads:
        one.start()

    barrier = pltpu.get_barrier_semaphore()
    for k in range(1, NZ):
        pl.semaphore_signal(barrier, inc=1, device_id={"tensor": lax.rem(t + 2 * k, TP)}, device_id_type=MESH)
    pl.semaphore_wait(barrier, NZ - 1)

    rows = CODEBOOKS * OWN
    x = depth_in[...].reshape(rows, DD)
    dn = (x * lax.rsqrt(jnp.mean(x * x, axis=-1, keepdims=True) + epsilon) * dgain[...]).astype(BF16)
    for i in range(3):
        loads[i].wait()
        proj[i] = dot(dn, wq[i]).astype(BF16)

    rq = lax.broadcasted_iota(jnp.int32, (rows, rows), 0)
    rk = lax.broadcasted_iota(jnp.int32, (rows, rows), 1)
    seen = (lax.rem(rq, OWN) == lax.rem(rk, OWN)) & (rq >= rk)
    low = lax.broadcasted_iota(jnp.int32, (rows, 128), 1) < DHEAD_DIM
    for j in range(DHEADS // 2):
        cols = slice(j * 128, (j + 1) * 128)
        q, k, v = proj[0, :, cols], proj[1, :, cols], proj[2, :, cols]
        parts = []
        for half in (low, jnp.logical_not(low)):
            scores = dot_t(jnp.where(half, q, jnp.zeros_like(q)), k) * DHEAD_DIM ** (-0.5)
            e = jnp.where(seen, jnp.exp(jnp.where(seen, scores, 0.0)), 0.0)
            w = (e / jnp.sum(e, axis=-1, keepdims=True)).astype(BF16)
            parts.append(dot(w, v))
        att[:, cols] = jnp.where(low, parts[0], parts[1]).astype(BF16)
    loads[3].wait()
    out = x + dot(att[...], wm[...])
    final = (out * lax.rsqrt(jnp.mean(out * out, axis=-1, keepdims=True) + epsilon) * fgain[...]).astype(BF16)
    fin[:, z] = final.reshape(CODEBOOKS, OWN, DD)

    def ring(right, s, block):
        books = pl.ds(0, CODEBOOKS) if s < 3 else (pl.ds(0, 4) if right else pl.ds(4, 4))
        view = fin.at[books, block]
        k = s + (0 if right else 4)
        return pltpu.make_async_remote_copy(
            src_ref=view, dst_ref=view, send_sem=ss.at[k], recv_sem=rs.at[k],
            device_id={"tensor": zup if right else zdown}, device_id_type=MESH)

    for s in range(4):
        if s:
            ring(True, s - 1, lax.rem(z + NZ - s, NZ)).wait_recv()
        ring(True, s, lax.rem(z + NZ - s, NZ)).start()
        if s:
            ring(False, s - 1, lax.rem(z + s, NZ)).wait_recv()
        ring(False, s, lax.rem(z + s, NZ)).start()
    far = lax.rem(z + 4, NZ)
    ring(True, 3, far).wait_recv()
    ring(False, 3, far).wait_recv()

    loads[4].wait()
    loads[5].wait()
    shared = OWN * NZ
    lanes = lax.broadcasted_iota(jnp.int32, (shared, 256), 1)
    spots = lax.broadcasted_iota(jnp.int32, (shared, 128), 1)
    total = jnp.zeros((shared, 128), F32)
    for c in range(CODEBOOKS):
        logits = dot(fin[c].reshape(shared, DD), wh[c])
        e = jnp.sum(jnp.exp(logits), axis=-1, keepdims=True)
        hit = jnp.sum(jnp.where(lanes == target[:, c:c + 1], logits, 0.0), axis=-1, keepdims=True)
        total = jnp.where(spots == c, e, total)
        total = jnp.where(spots == CODEBOOKS + c, hit, total)
    sums[...] = total.reshape(NZ, OWN, 128)

    def share(k, sender):
        to = lax.rem(z + k, NZ)
        return pltpu.make_async_remote_copy(
            src_ref=sums.at[to], dst_ref=got.at[sender], send_sem=tss.at[k], recv_sem=trs.at[k],
            device_id={"tensor": 2 * to + xl}, device_id_type=MESH)

    for k in range(1, NZ):
        share(k, z).start()
    got[z] = sums[z]
    for k in range(1, NZ):
        share(k, lax.rem(z + NZ - k, NZ)).wait_recv()
    both = got[0]
    for n in range(1, NZ):
        both = both + got[n]
    loss[...] = jnp.log(both[:, :CODEBOOKS]) - both[:, CODEBOOKS:2 * CODEBOOKS]
    for k in range(1, NZ):
        share(k, z).wait_send()
    for s in range(4):
        ring(True, s, z).wait_send()
        ring(False, s, z).wait_send()


def shards(hidden_in, attn_gain, qkv_weight, mix_weight, out_gain, depth_in_weight, text_table, code_tables,
           depth_gain, depth_qkv, depth_mix, final_gain, heads_weight, text_ids, codes):
    t = lax.axis_index("tensor")
    half = HEAD_DIM // 2
    angles = np.arange(FRAMES)[:, None] * 10000.0 ** (-np.arange(half) / half)[None, :]
    cosv = np.concatenate([np.cos(angles)] * 2, axis=1).astype(np.float32)
    sinv = np.concatenate([-np.sin(angles), np.sin(angles)], axis=1).astype(np.float32)
    count = text_table.shape[0]
    text = jnp.pad(text_table, ((0, -count % 128), (0, 0)))
    text_local = text_ids - t * count
    text_local = jnp.where((text_local >= 0) & (text_local < count), text_local, -1)[:, None]
    code_local = codes - t * code_tables.shape[1]

    vmem = pl.BlockSpec(memory_space=pltpu.VMEM)
    anym = pl.BlockSpec(memory_space=pl.ANY)
    dma = pltpu.SemaphoreType.DMA
    depth_in, dfull, hfull = pl.pallas_call(
        front,
        out_shape=(
            jax.ShapeDtypeStruct((CODEBOOKS, OWN, DD), F32),
            jax.ShapeDtypeStruct((3, DD, DD), BF16),
            jax.ShapeDtypeStruct((2, CODEBOOKS, DD, 128), BF16),
        ),
        in_specs=[vmem] * 12 + [anym] * 2,
        out_specs=(vmem, anym, anym),
        scratch_shapes=[
            pltpu.VMEM((4, DP, 256, 256), BF16),
            pltpu.VMEM((FRAMES, D), BF16),
            pltpu.VMEM((3, FRAMES, 256), F32),
            pltpu.VMEM((FRAMES, 256), BF16),
            pltpu.VMEM((TP, FRAMES, 256), BF16),
            pltpu.VMEM((TP, CODEBOOKS, OWN, DD), BF16),
            pltpu.VMEM((4, 2, CODEBOOKS, OWN, DD), BF16),
            pltpu.VMEM((3, 2, CODEBOOKS, OWN, DD), BF16),
            pltpu.VMEM((CODEBOOKS, OWN, DD), BF16),
            pltpu.VMEM((CODEBOOKS, OWN, DD), BF16),
            pltpu.VMEM((4, 2, FRAMES, 256), BF16),
            pltpu.VMEM((3, 2, FRAMES, 256), BF16),
            pltpu.VMEM((FRAMES, 256), BF16),
            pltpu.VMEM((FRAMES, 256), BF16),
            pltpu.VMEM((TP, OWN, DD), BF16),
            pltpu.VMEM((TP, OWN, DD), BF16),
            pltpu.VMEM((TP, OWN, 128), F32),
            pltpu.VMEM((TP, OWN, 128), F32),
            dma((5, 15)), dma((5, 15)),
            dma((8,)), dma((8,)),
            dma((8,)), dma((8,)),
            dma((2, TP)), dma((2, TP)),
            dma((2,)), dma((2,)),
            dma((2,)),
        ],
        compiler_params=pltpu.CompilerParams(
            collective_id=0, has_side_effects=True, vmem_limit_bytes=56 * 2**20),
        name="front",
    )(hidden_in, attn_gain[None], qkv_weight, mix_weight, out_gain[None], depth_in_weight, text, code_tables,
      text_local, code_local, cosv, sinv, depth_qkv, heads_weight)

    z, xl = t // 2, lax.rem(t, 2)
    target = lax.dynamic_index_in_dim(codes.reshape(NZ, 2, OWN, CODEBOOKS), xl, 1, keepdims=False)
    target = target.reshape(NZ * OWN, CODEBOOKS) - z * 256
    return pl.pallas_call(
        back,
        out_shape=jax.ShapeDtypeStruct((OWN, CODEBOOKS), F32),
        in_specs=[vmem, anym, vmem, anym, vmem, anym, vmem],
        out_specs=vmem,
        scratch_shapes=[
            pltpu.VMEM((3, DD, DD), BF16),
            pltpu.VMEM((DD, DD), BF16),
            pltpu.VMEM((CODEBOOKS, DD, 256), BF16),
            pltpu.VMEM((3, CODEBOOKS * OWN, DD), BF16),
            pltpu.VMEM((CODEBOOKS * OWN, DD), BF16),
            pltpu.VMEM((CODEBOOKS, NZ, OWN, DD), BF16),
            pltpu.VMEM((NZ, OWN, 128), F32),
            pltpu.VMEM((NZ, OWN, 128), F32),
            dma((6,)),
            dma((8,)), dma((8,)),
            dma((NZ,)), dma((NZ,)),
        ],
        compiler_params=pltpu.CompilerParams(
            collective_id=1, has_side_effects=True, vmem_limit_bytes=48 * 2**20),
        name="back",
    )(depth_in, dfull, depth_gain[None], depth_mix, final_gain[None], hfull, target)


def solution(mesh):
    in_specs = (
        P("dp", None),
        P(),
        P(None, "dp", "tensor"),
        P("tensor", "dp"),
        P(),
        P("tensor", None),
        P("tensor", None),
        P(None, "tensor", None),
        P(),
        P(None, "dp", None),
        P(),
        P(),
        P(None, None, "tensor"),
        P("dp"),
        P("dp", None),
    )
    out_specs = P(("dp", "tensor"), None)
    return jax.shard_map(shards, mesh=mesh, in_specs=in_specs, out_specs=out_specs, check_vma=False)
```

time: 647 us -> 176 us (0.27)
  waiting for transfers between devices: 432 us -> 0 us
  Pallas kernels: 0 us -> 169 us
  blocking collectives: 94.5 us -> 0 us
  local copies, waits for them, and re-layouts: 54.1 us -> 6 us
  matrix products: 29.1 us -> 0 us
  other arithmetic: 21.4 us -> 0.69 us
  between operations: 14.4 us -> 0.1 us
    all_gather x4 -> x0, waiting for transfers between devices: 280 us -> none  [the longest x1 99 us: shards(): final_all = lax.all_gather(final, 'tensor', axis=0, tiled=True)]
    pallas_call x0 -> x2, Pallas kernels: none -> 169 us  [the longest x1 128 us: shards(): pl.pallas_call(front, out_shape=(jax.ShapeDtypeStruct((CODEBOOKS, OWN, DD...]
    reduce_scatter x3 -> x0, waiting for transfers between devices: 150 us -> none  [the longest x1 100 us: arrive_embeds(): lax.psum_scatter(embeds.astype(jnp.bfloat16), 'tensor', scatter_dimension...]
    psum x1 -> x0, blocking collectives: 62.1 us -> none  [shards(): exp_total, target_total = lax.psum((exp_part, target_part), 'tensor')]
    gather x2 -> x0, local copies, waits for them, and re-layouts: 38.2 us -> none  [the longest x1 34.8 us: local_embeds(): code_found = code_tables[books, jnp.clip(code_local, 0, code_count - 1)]]
    unnamed x1 -> x0, blocking collectives: 32.4 us -> none
    dot_general x10 -> x0, matrix products: 29.1 us -> none  [the longest x1 5.6 us: shards(): jnp.einsum('rcd,cdv->rcv', final_all, heads_weight, preferred_element_typ...]
    convert_element_type x2 -> x0, local copies, waits for them, and re-layouts: 7.6 us -> none  [the longest x1 6.45 us: local_embeds(): code_found.astype(jnp.float32)]
  transfers between devices with their start and end apart: 7 -> 0, of which waited for: 7 -> 0; matrix products, arithmetic and copies ran while one was open for 12% -> 0% of each run, Pallas kernels for 0% -> 0%
where the time goes in v1:
time: 176 us
  Pallas kernels  169 us (96%)
  local copies, waits for them, and re-layouts  6 us (3%)
    pallas_call x1, Pallas kernels, shards(): pl.pallas_call(front, out_shape=(jax.ShapeDtypeStruct((CODEBOOKS, OWN, DD...  128 us
    pallas_call x1, Pallas kernels, shards(): pl.pallas_call(back, out_shape=jax.ShapeDtypeStruct((OWN, CODEBOOKS), F32...  40.9 us

profile of v1, /device:TPU:4, one launch (start us, length us, event | category | flops | bytes accessed | tf_op | source)
XLA Modules:
  0.0 175.5 jit_solution(2225235550728182385)
XLA Ops:
  0.0 0.0 copy-start.5
  0.0 0.0 copy-start.4
  0.0 3.1 %pad.4.text = bf16[1024,1024]{1,0:T(8,128)(2,1)} pad(bf16[1000,1024]{1,0:T(8,128)(2,1)} %param.23, bf16[]{:T(256)} %constant.16.clone.1), padding=0_24x0_0 | pad | bytes 4145154 | tf_op jit(solution)/shard_map/jit(_pad)/pad | solution.py:481
  3.1 0.0 copy-done.5
  3.1 0.8 copy.27.tid
  3.9 0.0 copy-done.4
  3.9 0.1 copy.25
  4.1 0.7 broadcast_subtract_fusion.code
  4.7 0.0 copy-start
  4.7 0.0 copy-start.2
  4.7 0.0 copy-start.3
  4.7 127.9 %front.1 = (f32[8,16,1024]{2,1,0:T(8,128)}, bf16[3,1024,1024]{2,1,0:T(8,128)(2,1)}, bf16[2,8,1024,128]{3,2,1,0:T(8,128)(2,1)}) custom-call(bf16[256,4096]{1,0:T(8,128)(2,1)} %hid.1, f32[1,4096]{1,0:T(1,128)} %bitcast.11, bf16[3,256,256]{2,1,0:T(8,128)(2,1)} %qkv.1, bf16[256,256]{1,0:T(8,128)(2,1)} %mix.1, f32[1,4096]{1,0:T(1,128)} %bitcast.12, ...), custom_call_target="tpu_custom_call" | custom-call | tf_op jit(solution)/shard_map/front/pallas_call | solution.py:489
  132.6 0.1 reshape.7
  132.8 0.1 copy.30
  132.9 0.0 copy-done
  132.9 0.0 copy-done.2
  132.9 0.0 copy-done.3
  133.0 0.0 copy-start.1
  133.0 1.0 copy-done.1
  134.0 40.9 %back.1 = f32[16,8]{1,0:T(8,128)S(1)} custom-call(f32[8,16,1024]{2,1,0:T(8,128)S(1)} %copy-done.1, bf16[3,1024,1024]{2,1,0:T(8,128)(2,1)} %get-tuple-element.9.dfull, f32[1,1024]{1,0:T(1,128)S(1)} %bitcast.9, bf16[1024,1024]{1,0:T(8,128)(2,1)S(1)} %copy-done, f32[1,1024]{1,0:T(1,128)S(1)} %bitcast.10, bf16[2,8,1024,128]{3,2,1,0:T(8,128)(2,1)} %get-tuple-element.10.hfull, ...), custom_call_target="tpu_custom_call" | custom-call | tf_op jit(solution)/shard_map/back/pallas_call | solution.py:533
  174.9 0.7 copy.29
  (3 shorter events, 0.0 us)
Async XLA Ops:
  0.0 3.1 %copy-start.5 = (s32[256]{0:T(256)S(1)}, s32[256]{0:T(256)}, u32[]{:S(2)}) copy-start(s32[256]{0:T(256)} %param.30) | copy-start | bytes 3076
  0.0 3.9 %copy-start.4 = (s32[256,8]{0,1:T(8,128)S(1)}, s32[256,8]{0,1:T(8,128)}, u32[]{:S(2)}) copy-start(s32[256,8]{0,1:T(8,128)} %param.31) | copy-start | bytes 24580
  4.7 128.2 %copy-start = (bf16[1024,1024]{1,0:T(8,128)(2,1)S(1)}, bf16[1024,1024]{1,0:T(8,128)(2,1)}, u32[]{:S(2)}) copy-start(bf16[1024,1024]{1,0:T(8,128)(2,1)} %dmix.1) | copy-start | bytes 6291460
  4.7 128.2 %copy-start.2 = (f32[1024]{0:T(1024)S(1)}, f32[1024]{0:T(1024)}, u32[]{:S(2)}) copy-start(f32[1024]{0:T(1024)} %param.25) | copy-start | bytes 12292
  4.7 128.2 %copy-start.3 = (f32[1024]{0:T(1024)S(1)}, f32[1024]{0:T(1024)}, u32[]{:S(2)}) copy-start(f32[1024]{0:T(1024)} %param.28) | copy-start | bytes 12292
  133.0 1.0 copy-start.1

commit v2 on v1

v2 whole, which is shorter than its diff:
```python
import functools

import jax
import jax.numpy as jnp
import numpy as np
from jax import lax
from jax.experimental import pallas as pl
from jax.experimental.pallas import tpu as pltpu
from jax.sharding import PartitionSpec as P

D = 4096
HEAD_DIM = 128
FRAMES = 256
DD = 1024
DHEADS = 16
DHEAD_DIM = 64
CODEBOOKS = 8
DP = 16
TP = 16
NZ = 8
OWN = 16
F32 = jnp.float32
BF16 = jnp.bfloat16
MESH = pl.DeviceIdType.MESH

epsilon = 1e-05

X0, R1, L1, R2, L2, R3, L3, C0 = range(8)


def dot(a, b):
    return jnp.dot(a, b, preferred_element_type=F32)


def dot_t(a, b):
    return lax.dot_general(a, b, (((1,), (1,)), ((), ())), preferred_element_type=F32)


class Places:
    def __init__(self):
        d = lax.axis_index("dp")
        t = lax.axis_index("tensor")
        self.d, self.t = d, t
        self.core = lax.rem(d, 2)
        self.xh = lax.rem(d // 2, 2)
        self.xl = lax.rem(t, 2)
        self.z = t // 2
        self.up = lax.rem(d + 4, 16)
        self.down = lax.rem(d + 12, 16)
        self.far = lax.rem(d + 8, 16)
        self.xstep = 2 - 4 * self.xh
        self.xpeer = d + self.xstep
        self.cstep = 1 - 2 * self.core
        self.cpeer = d + self.cstep
        self.xsib = t + 1 - 2 * self.xl
        self.zup = lax.rem(t + 2, 16)
        self.zdown = lax.rem(t + 14, 16)
        self.blocks = [d, self.xpeer, self.down, self.up, self.down + self.xstep,
                       self.up + self.xstep, self.far, self.far + self.xstep]


class Flow:
    def __init__(self, pos, own, block, send_sem, recv_sem):
        self.pos, self.own, self.block = pos, own, block
        self.ss, self.rs = send_sem, recv_sem

    def copy(self, kind, idx, dev, own=False):
        src = self.own if own else self.block(idx)
        return pltpu.make_async_remote_copy(
            src_ref=src, dst_ref=self.block(idx), send_sem=self.ss(kind), recv_sem=self.rs(kind),
            device_id={"dp": dev}, device_id_type=MESH)

    def start0(self):
        p = self.pos
        for kind, dev in ((X0, p.xpeer), (R1, p.up), (L1, p.down), (C0, p.cpeer)):
            self.copy(kind, p.d, dev, own=True).start()

    def core_in(self, n):
        p = self.pos
        self.copy(C0 + n, p.blocks[n] + p.cstep, p.cpeer).wait_recv()

    def got(self, kind):
        p = self.pos
        self.copy(kind, p.blocks[kind + 1], p.cpeer).wait_recv()

    def forward(self, kind, idx, dev):
        self.copy(kind, idx, dev).start()

    def to_core(self, kind):
        p = self.pos
        self.forward(C0 + kind + 1, p.blocks[kind + 1], p.cpeer)

    def stage1(self):
        p = self.pos
        self.got(X0)
        self.forward(R2, p.xpeer, p.up)
        self.forward(L2, p.xpeer, p.down)
        self.to_core(X0)
        self.got(R1)
        self.forward(R3, p.down, p.up)
        self.to_core(R1)
        self.got(L1)
        self.to_core(L1)

    def stage2(self):
        p = self.pos
        self.got(R2)
        self.to_core(R2)
        self.got(L2)
        self.forward(L3, p.up + p.xstep, p.down)
        self.to_core(L2)

    def stage3(self):
        self.got(R3)
        self.to_core(R3)
        self.got(L3)
        self.to_core(L3)

    def stage4(self):
        p = self.pos
        for n in range(8):
            self.core_in(n)

    def drain(self):
        p = self.pos
        for kind in range(15):
            self.copy(kind, p.d, p.cpeer).wait_send()


class Ring:
    def __init__(self, pos, own, slots, half, add, ss, rs):
        self.pos, self.own, self.slots, self.half, self.add = pos, own, slots, half, add
        self.ss, self.rs = ss, rs

    def dest(self, way, s):
        return lax.rem(self.pos.z + (4 - s if way == 0 else 4 + s), NZ)

    def copy(self, way, s):
        slots = self.slots[way]
        if s == 0:
            part = pl.ds(way * self.half, self.half)
            src, dst = self.own(self.dest(way, 0)).at[:, part], slots.at[0, :, part]
        else:
            src, dst = slots.at[s - 1], slots.at[s]
        k = 4 * way + s
        return pltpu.make_async_remote_copy(
            src_ref=src, dst_ref=dst, send_sem=self.ss.at[k], recv_sem=self.rs.at[k],
            device_id={"tensor": self.pos.zdown if way else self.pos.zup}, device_id_type=MESH)

    def clear(self):
        for way in range(2):
            rest = pl.ds((1 - way) * self.half, self.half)
            self.slots[way][0, :, rest] = jnp.zeros_like(self.slots[way][0, :, rest])

    def step(self, s):
        for way in range(2):
            if s:
                self.copy(way, s - 1).wait_recv()
                self.add(self.slots[way].at[s - 1], self.own(self.dest(way, s)))
            self.copy(way, s).start()

    def arrive(self):
        for way in range(2):
            self.copy(way, 3).wait_recv()

    def drain(self):
        for way in range(2):
            for s in range(4):
                self.copy(way, s).wait_send()


def layer(gain, ogain, text, ids, cosr, sinr, dgain, fgain, target,
          hid_h, qkv_h, mix_h, din_h, tabs_h, dqkv, dmix_h, heads,
          loss,
          hid, din, tabs, wall, normed, acc, att, part, emb, er, el, eo, ei, pr, pe, po, pi, bs, br,
          cs, cx, cr, wq, wm, wh, proj, datt, fin, sums, got,
          lsem, wss, wrs, ess, ers, pss, prs, bss, brs, xss, xrs, css, crs, hss, hrs, fss, frs, tss, trs):
    p = Places()
    d, t, z, xl = p.d, p.t, p.z, p.xl

    def block_of(f):
        return lambda i: wall.at[f, i]

    deep_block = lambda i: wq.at[:, pl.ds(pl.multiple_of(i * 64, 64), 64), :]
    own_lanes = pl.ds(pl.multiple_of(xl * 128, 128), 128)
    sib_lanes = pl.ds(pl.multiple_of((1 - xl) * 128, 128), 128)
    loads = [(qkv_h.at[0], wall.at[0, d]), (qkv_h.at[1], wall.at[1, d]), (qkv_h.at[2], wall.at[2, d]),
             (mix_h, wall.at[3, d]), (tabs_h, tabs), (hid_h, hid), (din_h, din), (dqkv, deep_block(d)),
             (dmix_h, wm), (heads, wh.at[:, :, own_lanes])]
    loads = [pltpu.make_async_copy(src, dst, lsem.at[n]) for n, (src, dst) in enumerate(loads)]
    for one in loads:
        one.start()

    def add_books(a, b):
        def one(n, carry):
            h, c = n // CODEBOOKS, lax.rem(n, CODEBOOKS)
            a[h, c] = a[h, c] + b[h, c]
            return carry

        lax.fori_loop(0, 2 * CODEBOOKS, one, 0)

    def add_rows(a, b):
        def one(n, carry):
            a[n] = (a[n].astype(F32) + b[n].astype(F32)).astype(BF16)
            return carry

        lax.fori_loop(0, 3, one, 0)

    ering = Ring(p, lambda i: emb.at[pl.ds(2 * i, 2)], (er, el), CODEBOOKS // 2, add_books, ess, ers)
    pring = Ring(p, lambda i: part.at[i], (pr, pe), 64, add_rows, pss, prs)
    ering.clear()
    pring.clear()

    barrier = pltpu.get_barrier_semaphore()
    for dev in (p.xpeer, p.up, p.down, p.cpeer):
        pl.semaphore_signal(barrier, inc=1, device_id={"dp": dev}, device_id_type=MESH)

    def greet(k, carry):
        pl.semaphore_signal(barrier, inc=1, device_id={"tensor": lax.rem(t + 2 * k, TP)}, device_id_type=MESH)
        return carry

    lax.fori_loop(1, NZ, greet, 0)
    pl.semaphore_signal(barrier, inc=1, device_id={"tensor": p.xsib}, device_id_type=MESH)
    pl.semaphore_wait(barrier, 4 + NZ)

    def flow(f):
        return Flow(p, wall.at[f, d], block_of(f), lambda k: wss.at[f, k], lambda k: wrs.at[f, k])

    def qkv_flows(act):
        def one(f, carry):
            act(flow(f))
            return carry

        lax.fori_loop(0, 3, one, 0)

    mixer = flow(3)
    deep = Flow(p, dqkv, deep_block, lambda k: wss.at[4, k], lambda k: wrs.at[4, k])
    for n in range(3):
        loads[n].wait()
    qkv_flows(lambda f: f.start0())

    idv = ids[...].astype(F32)
    pick = lax.broadcasted_iota(jnp.int32, idv.shape, 1)
    count = text.shape[0]
    whole = count // 128 * 128

    def named(c, start, width):
        want = jnp.sum(jnp.where(pick == c, idv, 0.0), axis=1, keepdims=True)
        lanes = lax.broadcasted_iota(jnp.int32, (FRAMES, width), 1).astype(F32) + start
        return (lanes == want).astype(BF16)

    found = dot(named(0, 0, whole), text[:whole])
    if count > whole:
        found = found + dot(named(0, whole, count - whole), text[whole:])
    emb[:, 0] = found.astype(BF16).reshape(TP, OWN, DD)
    loads[4].wait()

    def lookup(c, carry):
        emb[:, c] = dot(named(c, 0, 128), tabs[c - 1]).astype(BF16).reshape(TP, OWN, DD)
        return carry

    lax.fori_loop(1, CODEBOOKS, lookup, 0)
    ering.step(0)
    loads[5].wait()

    def norm_rows(n, carry):
        r = pl.ds(pl.multiple_of(n * 32, 32), 32)
        h = hid[r, :].astype(F32)
        scale = lax.rsqrt(jnp.mean(h * h, axis=-1, keepdims=True) + epsilon)
        normed[r, :] = (h * scale * gain[...]).astype(BF16)
        return carry

    lax.fori_loop(0, FRAMES // 32, norm_rows, 0)
    acc[...] = jnp.zeros_like(acc)

    def project(ns):
        for n in ns:
            def side(c, carry):
                @pl.when(c == 1)
                def _():
                    qkv_flows(lambda f: f.core_in(n))

                b = p.blocks[n] + c * p.cstep
                cols = normed[:, pl.ds(pl.multiple_of(b * 256, 256), 256)]

                def one(i, carry):
                    acc[i] += dot(cols, wall[i, b])
                    return carry

                return lax.fori_loop(0, 3, one, carry)

            lax.fori_loop(0, 2, side, 0)

    qkv_flows(lambda f: f.stage1())
    loads[3].wait()
    mixer.start0()
    project((0, 1, 2, 3))
    ering.step(1)
    qkv_flows(lambda f: f.stage2())
    mixer.stage1()
    loads[7].wait()
    deep.start0()
    project((4, 5))
    qkv_flows(lambda f: f.stage3())
    mixer.stage2()
    project((6, 7))
    ering.step(2)

    order_q = lax.broadcasted_iota(jnp.int32, (FRAMES, FRAMES), 0)
    order_k = lax.broadcasted_iota(jnp.int32, (FRAMES, FRAMES), 1)
    causal = order_q >= order_k

    def rotate(v):
        half = HEAD_DIM // 2
        swapped = jnp.concatenate([v[:, half:], v[:, :half]], axis=1)
        return (v * cosr[...] + swapped * sinr[...]).astype(BF16)

    def attend(h, carry):
        cols = pl.ds(pl.multiple_of(h * HEAD_DIM, HEAD_DIM), HEAD_DIM)
        q = rotate(acc[0, :, cols])
        k = rotate(acc[1, :, cols])
        v = acc[2, :, cols].astype(BF16)
        scores = dot_t(q, k) * HEAD_DIM ** (-0.5)
        e = jnp.where(causal, jnp.exp(jnp.where(causal, scores, 0.0)), 0.0)
        w = (e / jnp.sum(e, axis=-1, keepdims=True)).astype(BF16)
        att[:, cols] = dot(w, v).astype(BF16)
        return carry

    lax.fori_loop(0, 2, attend, 0)
    mixer.stage3()
    mixer.stage4()

    def cross(zz):
        return pltpu.make_async_remote_copy(
            src_ref=bs.at[zz], dst_ref=br.at[zz], send_sem=bss.at[zz], recv_sem=brs.at[zz],
            device_id={"tensor": p.xsib}, device_id_type=MESH)

    def near_far(n):
        step = (n + 1) // 2
        return lax.rem(z + 4 + jnp.where(lax.rem(n, 2) == 1, -step, step), NZ)

    def mixed(n, carry):
        zz = near_far(n)
        sib = dot(att[...], wall[3, 2 * zz + 1 - xl]).astype(BF16)
        bs[zz] = sib[128:]
        cross(zz).start()
        part[zz, 1 - xl] = sib[:128]
        mine = dot(att[...], wall[3, 2 * zz + xl]).astype(BF16)
        part[zz, xl] = mine[:128]
        part[zz, 2] = mine[128:]
        return carry

    lax.fori_loop(0, NZ, mixed, 0)
    ering.step(3)

    def crossed(n, carry):
        zz = near_far(n)
        cross(zz).wait_recv()
        part[zz, 2] = (part[zz, 2].astype(F32) + br[zz].astype(F32)).astype(BF16)
        return carry

    crossed(0, 0)
    pring.step(0)
    deep.stage1()
    lax.fori_loop(1, NZ, crossed, 0)
    pring.step(1)
    head_part = pl.ds(p.core * 4, 4)
    head_rest = pl.ds(4 - p.core * 4, 4)
    head_x = pltpu.make_async_remote_copy(
        src_ref=heads.at[head_part], dst_ref=wh.at[head_part, :, own_lanes], send_sem=hss.at[0],
        recv_sem=hrs.at[0], device_id={"tensor": p.xsib}, device_id_type=MESH)
    head_x.start()
    pring.step(2)
    deep.stage2()

    def swap(src, dst, k):
        return pltpu.make_async_remote_copy(
            src_ref=src, dst_ref=dst, send_sem=xss.at[k], recv_sem=xrs.at[k],
            device_id={"tensor": p.xsib}, device_id_type=MESH)

    ering.arrive()
    eo[...] = emb[2 * z + 1 - xl] + er[3, 1 - xl] + el[3, 1 - xl]
    swap(eo, ei, 0).start()
    pring.step(3)
    deep.stage3()
    pring.arrive()

    def total(h):
        return part[z, h].astype(F32) + pr[3, h].astype(F32) + pe[3, h].astype(F32)

    po[...] = total(1 - xl).astype(BF16)
    swap(po, pi, 1).start()
    loads[6].wait()
    cols = pl.ds(pl.multiple_of(t * 256, 256), 256)

    def context_part(rows, resid):
        at = slice(rows * 128, rows * 128 + 128)
        resid = resid + hid[at, cols].astype(F32)
        square = jnp.sum(resid * resid, axis=-1, keepdims=True)
        scaled = (resid * ogain[:, cols]).astype(BF16)
        at = slice(rows * 8, rows * 8 + 8)
        cs[at, :, :DD] = dot(scaled, din[...]).astype(BF16).reshape(8, OWN, DD)
        high = square.astype(BF16)
        low = (square - high.astype(F32)).astype(BF16)
        first = lax.broadcasted_iota(jnp.int32, (128, 128), 1) < 64
        both = jnp.where(first, high.astype(F32), low.astype(F32)).astype(BF16)
        cs[at, :, DD:] = both.reshape(8, OWN, 128)

    context_part(1, total(2))
    swap(po, pi, 1).wait_recv()
    context_part(0, total(xl) + pi[...].astype(F32))

    def over(zz):
        return pltpu.make_async_remote_copy(
            src_ref=cs.at[2 * zz + 1 - xl], dst_ref=cx.at[zz], send_sem=css.at[0, zz], recv_sem=crs.at[0, zz],
            device_id={"tensor": p.xsib}, device_id_type=MESH)

    def share(k, sender):
        to = lax.rem(z + k, NZ)
        return pltpu.make_async_remote_copy(
            src_ref=cs.at[2 * to + xl], dst_ref=cr.at[sender], send_sem=css.at[1, k], recv_sem=crs.at[1, k],
            device_id={"tensor": 2 * to + xl}, device_id_type=MESH)

    def start_over(n, carry):
        over(near_far(n)).start()
        return carry

    lax.fori_loop(0, NZ, start_over, 0)

    def squares(v):
        hl = v[:, DD:].astype(F32)
        return hl[:, :1] + hl[:, 64:65]

    def pair_sum(n, carry):
        zz = near_far(n)
        over(zz).wait_recv()
        mine, theirs = cs[2 * zz + xl], cx[zz]
        cs[2 * zz + xl, :, :DD] = (mine[:, :DD].astype(F32) + theirs[:, :DD].astype(F32)).astype(BF16)
        square = squares(mine) + squares(theirs)
        high = square.astype(BF16)
        low = (square - high.astype(F32)).astype(BF16)
        first = lax.broadcasted_iota(jnp.int32, (OWN, 128), 1) < 64
        cs[2 * zz + xl, :, DD:] = jnp.where(first, high.astype(F32), low.astype(F32)).astype(BF16)
        return carry

    def pass_on(n, carry):
        pair_sum(n, 0)
        share(lax.rem(near_far(n) - z + NZ, NZ), z).start()
        return carry

    lax.fori_loop(0, NZ - 1, pass_on, 0)
    pair_sum(NZ - 1, 0)
    swap(eo, ei, 0).wait_recv()
    cr[z] = cs[2 * z + xl]

    def take(k, carry):
        share(k, lax.rem(z + NZ - k, NZ)).wait_recv()
        return carry

    lax.fori_loop(1, NZ, take, 0)

    def gathered(n, carry):
        context, square = carry
        v = cr[n]
        return context + v[:, :DD].astype(F32), square + squares(v)

    context, square = lax.fori_loop(0, NZ, gathered, (jnp.zeros((OWN, DD), F32), jnp.zeros((OWN, 1), F32)))
    context = context * lax.rsqrt(square / D + epsilon)
    embeds = emb[2 * z + xl].astype(F32) + er[3, xl].astype(F32) + el[3, xl].astype(F32) + ei[...].astype(F32)

    rows = CODEBOOKS * OWN
    x = (context[None] + embeds).reshape(rows, DD)
    dn = (x * lax.rsqrt(jnp.mean(x * x, axis=-1, keepdims=True) + epsilon) * dgain[...]).astype(BF16)
    deep.stage4()

    def dproject(i, carry):
        proj[i] = dot(dn, wq[i]).astype(BF16)
        return carry

    lax.fori_loop(0, 3, dproject, 0)
    head_x_in = pltpu.make_async_remote_copy(
        src_ref=wh.at[head_part, :, sib_lanes], dst_ref=wh.at[head_part, :, sib_lanes], send_sem=hss.at[1],
        recv_sem=hrs.at[0], device_id={"dp": p.cpeer}, device_id_type=MESH)
    head_x_in.wait_recv()
    head_c = pltpu.make_async_remote_copy(
        src_ref=wh.at[head_part, :, sib_lanes], dst_ref=wh.at[head_part, :, sib_lanes], send_sem=hss.at[1],
        recv_sem=hrs.at[1], device_id={"dp": p.cpeer}, device_id_type=MESH)
    head_c.start()

    rq = lax.broadcasted_iota(jnp.int32, (rows, rows), 0)
    rk = lax.broadcasted_iota(jnp.int32, (rows, rows), 1)
    seen = (lax.rem(rq, OWN) == lax.rem(rk, OWN)) & (rq >= rk)
    low_half = lax.broadcasted_iota(jnp.int32, (rows, 128), 1) < DHEAD_DIM

    def dattend(j, carry):
        cols = pl.ds(pl.multiple_of(j * 128, 128), 128)
        q, k, v = proj[0, :, cols], proj[1, :, cols], proj[2, :, cols]
        parts = []
        for half in (low_half, jnp.logical_not(low_half)):
            scores = dot_t(jnp.where(half, q, jnp.zeros_like(q)), k) * DHEAD_DIM ** (-0.5)
            e = jnp.where(seen, jnp.exp(jnp.where(seen, scores, 0.0)), 0.0)
            w = (e / jnp.sum(e, axis=-1, keepdims=True)).astype(BF16)
            parts.append(dot(w, v))
        datt[:, cols] = jnp.where(low_half, parts[0], parts[1]).astype(BF16)
        return carry

    lax.fori_loop(0, DHEADS // 2, dattend, 0)
    loads[8].wait()
    out = x + dot(datt[...], wm[...])
    final = (out * lax.rsqrt(jnp.mean(out * out, axis=-1, keepdims=True) + epsilon) * fgain[...]).astype(BF16)
    fin[:, z] = final.reshape(CODEBOOKS, OWN, DD)

    def ring(way, s, block):
        books = pl.ds(0, CODEBOOKS) if s < 3 else pl.ds(4 * way, 4)
        view = fin.at[books, block]
        return pltpu.make_async_remote_copy(
            src_ref=view, dst_ref=view, send_sem=fss.at[4 * way + s], recv_sem=frs.at[4 * way + s],
            device_id={"tensor": p.zdown if way else p.zup}, device_id_type=MESH)

    for s in range(4):
        for way in range(2):
            block = lax.rem(z + (s if way else NZ - s), NZ)
            if s:
                ring(way, s - 1, block).wait_recv()
            ring(way, s, block).start()
    far = lax.rem(z + 4, NZ)
    ring(0, 3, far).wait_recv()
    ring(1, 3, far).wait_recv()

    loads[9].wait()
    pltpu.make_async_remote_copy(
        src_ref=wh.at[head_rest, :, sib_lanes], dst_ref=wh.at[head_rest, :, sib_lanes], send_sem=hss.at[1],
        recv_sem=hrs.at[1], device_id={"dp": p.cpeer}, device_id_type=MESH).wait_recv()
    shared = OWN * NZ
    lanes = lax.broadcasted_iota(jnp.int32, (shared, 256), 1).astype(F32)
    spots = lax.broadcasted_iota(jnp.int32, (shared, 128), 1)
    goal = target[...].astype(F32)
    books = lax.broadcasted_iota(jnp.int32, goal.shape, 1)

    def book(c, total):
        logits = dot(fin[c].reshape(shared, DD), wh[c])
        e = jnp.sum(jnp.exp(logits), axis=-1, keepdims=True)
        want = jnp.sum(jnp.where(books == c, goal, 0.0), axis=1, keepdims=True)
        hit = jnp.sum(jnp.where(lanes == want, logits, 0.0), axis=-1, keepdims=True)
        total = jnp.where(spots == c, e, total)
        return jnp.where(spots == CODEBOOKS + c, hit, total)

    sums[...] = lax.fori_loop(0, CODEBOOKS, book, jnp.zeros((shared, 128), F32)).reshape(NZ, OWN, 128)

    def reply(k, sender):
        to = lax.rem(z + k, NZ)
        return pltpu.make_async_remote_copy(
            src_ref=sums.at[to], dst_ref=got.at[sender], send_sem=tss.at[k], recv_sem=trs.at[k],
            device_id={"tensor": 2 * to + xl}, device_id_type=MESH)

    def start_reply(k, carry):
        reply(k, z).start()
        return carry

    def take_reply(k, carry):
        reply(k, lax.rem(z + NZ - k, NZ)).wait_recv()
        return carry

    lax.fori_loop(1, NZ, start_reply, 0)
    got[z] = sums[z]
    lax.fori_loop(1, NZ, take_reply, 0)
    both = got[0]
    for n in range(1, NZ):
        both = both + got[n]
    loss[...] = jnp.log(both[:, :CODEBOOKS]) - both[:, CODEBOOKS:2 * CODEBOOKS]

    qkv_flows(lambda f: f.drain())
    mixer.drain()
    deep.drain()
    ering.drain()
    pring.drain()
    swap(eo, ei, 0).wait_send()
    swap(po, pi, 1).wait_send()
    head_x.wait_send()
    head_c.wait_send()

    def sent(k, carry):
        cross(k).wait_send()
        over(k).wait_send()
        return carry

    def sent_far(k, carry):
        share(k, z).wait_send()
        reply(k, z).wait_send()
        return carry

    lax.fori_loop(0, NZ, sent, 0)
    lax.fori_loop(1, NZ, sent_far, 0)
    for s in range(4):
        for way in range(2):
            ring(way, s, z).wait_send()


def shards(hidden_in, attn_gain, qkv_weight, mix_weight, out_gain, depth_in_weight, text_table, code_tables,
           depth_gain, depth_qkv, depth_mix, final_gain, heads_weight, text_ids, codes):
    t = lax.axis_index("tensor")
    half = HEAD_DIM // 2
    angles = np.arange(FRAMES)[:, None] * 10000.0 ** (-np.arange(half) / half)[None, :]
    cosv = np.concatenate([np.cos(angles)] * 2, axis=1).astype(np.float32)
    sinv = np.concatenate([-np.sin(angles), np.sin(angles)], axis=1).astype(np.float32)
    ids = jnp.concatenate(
        [text_ids[:, None] - t * text_table.shape[0], codes[:, :CODEBOOKS - 1] - t * code_tables.shape[1]], axis=1)
    z, xl = t // 2, lax.rem(t, 2)
    target = lax.dynamic_index_in_dim(codes.reshape(NZ, 2, OWN, CODEBOOKS), xl, 1, keepdims=False)
    target = target.reshape(NZ * OWN, CODEBOOKS) - z * 256

    vmem = pl.BlockSpec(memory_space=pltpu.VMEM)
    anym = pl.BlockSpec(memory_space=pl.ANY)
    dma = pltpu.SemaphoreType.DMA
    b16 = lambda *shape: pltpu.VMEM(shape, BF16)
    f32 = lambda *shape: pltpu.VMEM(shape, F32)
    wide = DD + 128
    return pl.pallas_call(
        layer,
        out_shape=jax.ShapeDtypeStruct((OWN, CODEBOOKS), F32),
        in_specs=[vmem] * 9 + [anym] * 8,
        out_specs=vmem,
        scratch_shapes=[
            b16(FRAMES, D), b16(256, DD), b16(CODEBOOKS - 1, 128, DD),
            b16(4, DP, 256, 256), b16(FRAMES, D), f32(3, FRAMES, 256), b16(FRAMES, 256),
            b16(NZ, 3, 128, 256),
            b16(TP, CODEBOOKS, OWN, DD),
            b16(4, 2, CODEBOOKS, OWN, DD), b16(4, 2, CODEBOOKS, OWN, DD),
            b16(CODEBOOKS, OWN, DD), b16(CODEBOOKS, OWN, DD),
            b16(4, 3, 128, 256), b16(4, 3, 128, 256), b16(128, 256), b16(128, 256),
            b16(NZ, 128, 256), b16(NZ, 128, 256),
            b16(TP, OWN, wide), b16(NZ, OWN, wide), b16(NZ, OWN, wide),
            b16(3, DD, DD), b16(DD, DD), b16(CODEBOOKS, DD, 256),
            b16(3, CODEBOOKS * OWN, DD), b16(CODEBOOKS * OWN, DD),
            b16(CODEBOOKS, NZ, OWN, DD), f32(NZ, OWN, 128), f32(NZ, OWN, 128),
            dma((10,)),
            dma((5, 15)), dma((5, 15)),
            dma((8,)), dma((8,)),
            dma((8,)), dma((8,)),
            dma((NZ,)), dma((NZ,)),
            dma((2,)), dma((2,)),
            dma((2, NZ)), dma((2, NZ)),
            dma((2,)), dma((2,)),
            dma((8,)), dma((8,)),
            dma((NZ,)), dma((NZ,)),
        ],
        compiler_params=pltpu.CompilerParams(
            collective_id=0, has_side_effects=True, vmem_limit_bytes=60 * 2**20),
        name="layer",
    )(attn_gain[None], out_gain[None], text_table, ids, cosv, sinv, depth_gain[None], final_gain[None], target,
      hidden_in, qkv_weight, mix_weight, depth_in_weight, code_tables, depth_qkv, depth_mix, heads_weight)


def solution(mesh):
    in_specs = (
        P("dp", None),
        P(),
        P(None, "dp", "tensor"),
        P("tensor", "dp"),
        P(),
        P("tensor", None),
        P("tensor", None),
        P(None, "tensor", None),
        P(),
        P(None, "dp", None),
        P(),
        P(),
        P(None, None, "tensor"),
        P("dp"),
        P("dp", None),
    )
    out_specs = P(("dp", "tensor"), None)
    return jax.shard_map(shards, mesh=mesh, in_specs=in_specs, out_specs=out_specs, check_vma=False)
```

time: 176 us -> 172 us (0.977)
  Pallas kernels: 169 us -> 166 us
  local copies, waits for them, and re-layouts: 6 us -> 3.07 us
    pad x1 -> x0, local copies, waits for them, and re-layouts: 3.1 us -> none  [shards(): text = jnp.pad(text_table, ((0, -count % 128), (0, 0)))]
    pallas_call x2 -> x1, Pallas kernels: 169 us -> 166 us  [shards(): pl.pallas_call(layer, out_shape=jax.ShapeDtypeStruct((OWN, CODEBOOKS), F3...]
where the time goes in v2:
time: 172 us
  Pallas kernels  166 us (97%)
  local copies, waits for them, and re-layouts  3.07 us (2%)
  other arithmetic  2.02 us (1%)
    pallas_call x1, Pallas kernels, shards(): pl.pallas_call(layer, out_shape=jax.ShapeDtypeStruct((OWN, CODEBOOKS), F3...  166 us

profile of v2, /device:TPU:4, one launch (start us, length us, event | category | flops | bytes accessed | tf_op | source)
XLA Modules:
  0.0 171.6 jit_solution(13590426009881162875)
XLA Ops:
  0.0 0.7 broadcast_subtract_fusion.1
  0.7 0.7 slice_subtract_fusion
  1.4 0.8 reshape.8
  2.3 0.1 copy.30
  2.4 0.6 broadcast_subtract_fusion
  3.0 0.8 copy.28.ids
  3.8 166.5 %layer.1 = f32[16,8]{1,0:T(8,128)} custom-call(f32[1,4096]{1,0:T(1,128)} %bitcast.9, f32[1,4096]{1,0:T(1,128)} %bitcast.10, bf16[1000,1024]{1,0:T(8,128)(2,1)} %text.1, s32[256,8]{1,0:T(8,128)} %copy.28.ids, f32[256,128]{1,0:T(8,128)} %constant.33.clone.cosr, f32[256,128]{1,0:T(8,128)} %constant.34.clone.sinr, f32[1,1024]{1,0:T(1,128)} %bitcast.11, ...), custom_call_target="tpu_custom_call" | custom-call | tf_op jit(solution)/shard_map/layer/pallas_call | solution.py:618
  170.2 1.4 copy.29
  (2 shorter events, 0.0 us)

commit v3 on v2

--- a/solution.py
+++ b/solution.py
@@ -169,11 +169,11 @@
                 self.copy(way, s).wait_send()
 
 
-def layer(gain, ogain, text, ids, cosr, sinr, dgain, fgain, target,
+def layer(gain, ogain, text, tid, code, cosr, sinr, dgain, fgain,
           hid_h, qkv_h, mix_h, din_h, tabs_h, dqkv, dmix_h, heads,
           loss,
-          hid, din, tabs, wall, normed, acc, att, part, emb, er, el, eo, ei, pr, pe, po, pi, bs, br,
-          cs, cx, cr, wq, wm, wh, proj, datt, fin, sums, got,
+          hid, hown, din, tabs, goal, wall, normed, acc, att, part, emb, er, el, eo, ei, pr, pe, po, pi, bs, br,
+          cs, cr, xin, wq, wm, wh, proj, datt, fin, sums, got,
           lsem, wss, wrs, ess, ers, pss, prs, bss, brs, xss, xrs, css, crs, hss, hrs, fss, frs, tss, trs):
     p = Places()
     d, t, z, xl = p.d, p.t, p.z, p.xl
@@ -185,7 +185,7 @@
     own_lanes = pl.ds(pl.multiple_of(xl * 128, 128), 128)
     sib_lanes = pl.ds(pl.multiple_of((1 - xl) * 128, 128), 128)
     loads = [(qkv_h.at[0], wall.at[0, d]), (qkv_h.at[1], wall.at[1, d]), (qkv_h.at[2], wall.at[2, d]),
-             (mix_h, wall.at[3, d]), (tabs_h, tabs), (hid_h, hid), (din_h, din), (dqkv, deep_block(d)),
+             (mix_h, wall.at[3, d]), (tabs_h, tabs), (hid_h, hid), (din_h, din.at[xl]), (dqkv, deep_block(d)),
              (dmix_h, wm), (heads, wh.at[:, :, own_lanes])]
     loads = [pltpu.make_async_copy(src, dst, lsem.at[n]) for n, (src, dst) in enumerate(loads)]
     for one in loads:
@@ -193,11 +193,11 @@
 
     def add_books(a, b):
         def one(n, carry):
-            h, c = n // CODEBOOKS, lax.rem(n, CODEBOOKS)
+            h, c = n // 4, lax.rem(n, 4)
             a[h, c] = a[h, c] + b[h, c]
             return carry
 
-        lax.fori_loop(0, 2 * CODEBOOKS, one, 0)
+        lax.fori_loop(0, 8, one, 0)
 
     def add_rows(a, b):
         def one(n, carry):
@@ -206,9 +206,14 @@
 
         lax.fori_loop(0, 3, one, 0)
 
-    ering = Ring(p, lambda i: emb.at[pl.ds(2 * i, 2)], (er, el), CODEBOOKS // 2, add_books, ess, ers)
+    def ering_of(n):
+        books = pl.ds(4 * n, 4)
+        return Ring(p, lambda i: emb.at[pl.ds(2 * i, 2), books], (er.at[n], el.at[n]), 2, add_books, ess.at[n], ers.at[n])
+
+    erings = [ering_of(n) for n in range(2)]
     pring = Ring(p, lambda i: part.at[i], (pr, pe), 64, add_rows, pss, prs)
-    ering.clear()
+    erings[0].clear()
+    erings[1].clear()
     pring.clear()
 
     barrier = pltpu.get_barrier_semaphore()
@@ -239,28 +244,35 @@
         loads[n].wait()
     qkv_flows(lambda f: f.start0())
 
-    idv = ids[...].astype(F32)
-    pick = lax.broadcasted_iota(jnp.int32, idv.shape, 1)
+    codev = code[...].astype(F32)
+    pick = lax.broadcasted_iota(jnp.int32, codev.shape, 1)
     count = text.shape[0]
     whole = count // 128 * 128
-
-    def named(c, start, width):
-        want = jnp.sum(jnp.where(pick == c, idv, 0.0), axis=1, keepdims=True)
+    square_r = lax.broadcasted_iota(jnp.int32, (128, 128), 0)
+    square_c = lax.broadcasted_iota(jnp.int32, (128, 128), 1)
+    halves = [jnp.sum(jnp.where(square_r == square_c, jnp.broadcast_to(tid[h:h + 1].astype(F32), (128, 128)), 0.0),
+                      axis=1, keepdims=True) for h in range(2)]
+    text_want = jnp.concatenate(halves, axis=0) - (t * count).astype(F32)
+
+    def named(want, start, width):
         lanes = lax.broadcasted_iota(jnp.int32, (FRAMES, width), 1).astype(F32) + start
         return (lanes == want).astype(BF16)
 
-    found = dot(named(0, 0, whole), text[:whole])
+    found = dot(named(text_want, 0, whole), text[:whole])
     if count > whole:
-        found = found + dot(named(0, whole, count - whole), text[whole:])
+        found = found + dot(named(text_want, whole, count - whole), text[whole:])
     emb[:, 0] = found.astype(BF16).reshape(TP, OWN, DD)
     loads[4].wait()
 
     def lookup(c, carry):
-        emb[:, c] = dot(named(c, 0, 128), tabs[c - 1]).astype(BF16).reshape(TP, OWN, DD)
-        return carry
-
-    lax.fori_loop(1, CODEBOOKS, lookup, 0)
-    ering.step(0)
+        want = jnp.sum(jnp.where(pick == c - 1, codev, 0.0), axis=1, keepdims=True) - (t * 128).astype(F32)
+        emb[:, c] = dot(named(want, 0, 128), tabs[c - 1]).astype(BF16).reshape(TP, OWN, DD)
+        return carry
+
+    lax.fori_loop(1, 4, lookup, 0)
+    erings[0].step(0)
+    lax.fori_loop(4, CODEBOOKS, lookup, 0)
+    erings[1].step(0)
     loads[5].wait()
 
     def norm_rows(n, carry):
@@ -271,40 +283,61 @@
         return carry
 
     lax.fori_loop(0, FRAMES // 32, norm_rows, 0)
-    acc[...] = jnp.zeros_like(acc)
-
-    def project(ns):
+
+    def side_rows(n, carry):
+        frames = pl.ds(pl.multiple_of(n * 32 + xl * 16, 16), OWN)
+        to = pl.ds(pl.multiple_of(n * 16, 16), OWN)
+        hown[to, :] = hid[frames, pl.ds(pl.multiple_of(z * 512, 512), 512)]
+        goal[to, :] = code[frames, :]
+        return carry
+
+    lax.fori_loop(0, NZ, side_rows, 0)
+    def project(ns, first=False):
         for n in ns:
-            def side(c, carry):
-                @pl.when(c == 1)
-                def _():
-                    qkv_flows(lambda f: f.core_in(n))
-
-                b = p.blocks[n] + c * p.cstep
-                cols = normed[:, pl.ds(pl.multiple_of(b * 256, 256), 256)]
-
-                def one(i, carry):
-                    acc[i] += dot(cols, wall[i, b])
-                    return carry
-
-                return lax.fori_loop(0, 3, one, carry)
-
-            lax.fori_loop(0, 2, side, 0)
-
-    qkv_flows(lambda f: f.stage1())
+            for f in range(3):
+                flow(f).core_in(n)
+        y = p.blocks[ns[0]] // 4
+        cols = normed[:, pl.ds(pl.multiple_of(y * 1024, 1024), 1024)]
+
+        def one(i, carry):
+            got_one = dot(cols, wall[i, pl.ds(4 * y, 4)].reshape(1024, 256))
+            acc[i] = got_one if first else acc[i] + got_one
+            return carry
+
+        lax.fori_loop(0, 3, one, 0)
+
+    flow(0).stage1()
+    erings[0].step(1)
+    flow(1).stage1()
+    erings[1].step(1)
+    flow(2).stage1()
     loads[3].wait()
     mixer.start0()
-    project((0, 1, 2, 3))
-    ering.step(1)
-    qkv_flows(lambda f: f.stage2())
+    din_x = pltpu.make_async_remote_copy(
+        src_ref=din_h, dst_ref=din.at[xl], send_sem=hss.at[2], recv_sem=hrs.at[2],
+        device_id={"tensor": p.xsib}, device_id_type=MESH)
+    din_x.start()
+    head_part = pl.ds(p.core * 4, 4)
+    head_rest = pl.ds(4 - p.core * 4, 4)
+    head_x = pltpu.make_async_remote_copy(
+        src_ref=heads.at[head_part], dst_ref=wh.at[head_part, :, own_lanes], send_sem=hss.at[0],
+        recv_sem=hrs.at[0], device_id={"tensor": p.xsib}, device_id_type=MESH)
+    project((0, 1), True)
+    flow(0).stage2()
+    erings[0].step(2)
+    flow(1).stage2()
+    flow(2).stage2()
     mixer.stage1()
+    erings[1].step(2)
+    project((2, 4))
+    project((3, 5))
+    for f in range(3):
+        flow(f).stage3()
+    mixer.stage2()
     loads[7].wait()
     deep.start0()
-    project((4, 5))
-    qkv_flows(lambda f: f.stage3())
-    mixer.stage2()
+    erings[0].step(3)
     project((6, 7))
-    ering.step(2)
 
     order_q = lax.broadcasted_iota(jnp.int32, (FRAMES, FRAMES), 0)
     order_k = lax.broadcasted_iota(jnp.int32, (FRAMES, FRAMES), 1)
@@ -323,10 +356,13 @@
         scores = dot_t(q, k) * HEAD_DIM ** (-0.5)
         e = jnp.where(causal, jnp.exp(jnp.where(causal, scores, 0.0)), 0.0)
         w = (e / jnp.sum(e, axis=-1, keepdims=True)).astype(BF16)
-        att[:, cols] = dot(w, v).astype(BF16)
+        mixed_rows = dot(w, v).astype(BF16).reshape(NZ, 2, OWN, HEAD_DIM)
+        for side in range(2):
+            att[side * 128:side * 128 + 128, cols] = mixed_rows[:, side].reshape(128, HEAD_DIM)
         return carry
 
     lax.fori_loop(0, 2, attend, 0)
+    erings[1].step(3)
     mixer.stage3()
     mixer.stage4()
 
@@ -341,17 +377,17 @@
 
     def mixed(n, carry):
         zz = near_far(n)
-        sib = dot(att[...], wall[3, 2 * zz + 1 - xl]).astype(BF16)
-        bs[zz] = sib[128:]
+        second = wall[3, 2 * zz + 1]
+        bs[zz] = dot(att[pl.ds(pl.multiple_of(128 - 128 * xl, 128), 128), :], second).astype(BF16)
         cross(zz).start()
-        part[zz, 1 - xl] = sib[:128]
-        mine = dot(att[...], wall[3, 2 * zz + xl]).astype(BF16)
-        part[zz, xl] = mine[:128]
-        part[zz, 2] = mine[128:]
+        part[zz, 2] = dot(att[pl.ds(pl.multiple_of(128 * xl, 128), 128), :], second).astype(BF16)
+        one = dot(att[...], wall[3, 2 * zz]).astype(BF16)
+        part[zz, 0] = one[:128]
+        part[zz, 1] = one[128:]
         return carry
 
     lax.fori_loop(0, NZ, mixed, 0)
-    ering.step(3)
+    head_x.start()
 
     def crossed(n, carry):
         zz = near_far(n)
@@ -361,28 +397,22 @@
 
     crossed(0, 0)
     pring.step(0)
-    deep.stage1()
     lax.fori_loop(1, NZ, crossed, 0)
     pring.step(1)
-    head_part = pl.ds(p.core * 4, 4)
-    head_rest = pl.ds(4 - p.core * 4, 4)
-    head_x = pltpu.make_async_remote_copy(
-        src_ref=heads.at[head_part], dst_ref=wh.at[head_part, :, own_lanes], send_sem=hss.at[0],
-        recv_sem=hrs.at[0], device_id={"tensor": p.xsib}, device_id_type=MESH)
-    head_x.start()
     pring.step(2)
-    deep.stage2()
+    deep.stage1()
 
     def swap(src, dst, k):
         return pltpu.make_async_remote_copy(
             src_ref=src, dst_ref=dst, send_sem=xss.at[k], recv_sem=xrs.at[k],
             device_id={"tensor": p.xsib}, device_id_type=MESH)
 
-    ering.arrive()
-    eo[...] = emb[2 * z + 1 - xl] + er[3, 1 - xl] + el[3, 1 - xl]
+    pring.step(3)
+    for n in range(2):
+        erings[n].arrive()
+        mine = pl.ds(4 * n, 4)
+        eo[mine] = emb[2 * z + 1 - xl, mine] + er[n, 3, 1 - xl] + el[n, 3, 1 - xl]
     swap(eo, ei, 0).start()
-    pring.step(3)
-    deep.stage3()
     pring.arrive()
 
     def total(h):
@@ -391,67 +421,41 @@
     po[...] = total(1 - xl).astype(BF16)
     swap(po, pi, 1).start()
     loads[6].wait()
-    cols = pl.ds(pl.multiple_of(t * 256, 256), 256)
-
-    def context_part(rows, resid):
-        at = slice(rows * 128, rows * 128 + 128)
-        resid = resid + hid[at, cols].astype(F32)
-        square = jnp.sum(resid * resid, axis=-1, keepdims=True)
-        scaled = (resid * ogain[:, cols]).astype(BF16)
-        at = slice(rows * 8, rows * 8 + 8)
-        cs[at, :, :DD] = dot(scaled, din[...]).astype(BF16).reshape(8, OWN, DD)
-        high = square.astype(BF16)
-        low = (square - high.astype(F32)).astype(BF16)
-        first = lax.broadcasted_iota(jnp.int32, (128, 128), 1) < 64
-        both = jnp.where(first, high.astype(F32), low.astype(F32)).astype(BF16)
-        cs[at, :, DD:] = both.reshape(8, OWN, 128)
-
-    context_part(1, total(2))
+    din_x.wait_recv()
+
+    def scale_cols(b, summed):
+        resid = summed + hown[:, b * 256:b * 256 + 256].astype(F32)
+        gains = ogain[:, pl.ds(pl.multiple_of(z * 512 + b * 256, 256), 256)]
+        return jnp.sum(resid * resid, axis=-1, keepdims=True), dot((resid * gains).astype(BF16), din[b])
+
+    square, context = scale_cols(1, total(2))
     swap(po, pi, 1).wait_recv()
-    context_part(0, total(xl) + pi[...].astype(F32))
-
-    def over(zz):
-        return pltpu.make_async_remote_copy(
-            src_ref=cs.at[2 * zz + 1 - xl], dst_ref=cx.at[zz], send_sem=css.at[0, zz], recv_sem=crs.at[0, zz],
-            device_id={"tensor": p.xsib}, device_id_type=MESH)
+    square_b, context_b = scale_cols(0, total(xl) + pi[...].astype(F32))
+    square = square + square_b
+    cs[:, :, :DD] = (context + context_b).astype(BF16).reshape(NZ, OWN, DD)
+    high = square.astype(BF16)
+    low = (square - high.astype(F32)).astype(BF16)
+    first = lax.broadcasted_iota(jnp.int32, (128, 128), 1) < 64
+    both = jnp.where(first, high.astype(F32), low.astype(F32)).astype(BF16)
+    cs[:, :, DD:] = both.reshape(NZ, OWN, 128)
 
     def share(k, sender):
         to = lax.rem(z + k, NZ)
         return pltpu.make_async_remote_copy(
-            src_ref=cs.at[2 * to + xl], dst_ref=cr.at[sender], send_sem=css.at[1, k], recv_sem=crs.at[1, k],
+            src_ref=cs.at[to], dst_ref=cr.at[sender], send_sem=css.at[k], recv_sem=crs.at[k],
             device_id={"tensor": 2 * to + xl}, device_id_type=MESH)
 
-    def start_over(n, carry):
-        over(near_far(n)).start()
-        return carry
-
-    lax.fori_loop(0, NZ, start_over, 0)
-
-    def squares(v):
-        hl = v[:, DD:].astype(F32)
-        return hl[:, :1] + hl[:, 64:65]
-
-    def pair_sum(n, carry):
-        zz = near_far(n)
-        over(zz).wait_recv()
-        mine, theirs = cs[2 * zz + xl], cx[zz]
-        cs[2 * zz + xl, :, :DD] = (mine[:, :DD].astype(F32) + theirs[:, :DD].astype(F32)).astype(BF16)
-        square = squares(mine) + squares(theirs)
-        high = square.astype(BF16)
-        low = (square - high.astype(F32)).astype(BF16)
-        first = lax.broadcasted_iota(jnp.int32, (OWN, 128), 1) < 64
-        cs[2 * zz + xl, :, DD:] = jnp.where(first, high.astype(F32), low.astype(F32)).astype(BF16)
-        return carry
-
-    def pass_on(n, carry):
-        pair_sum(n, 0)
+    def give(n, carry):
         share(lax.rem(near_far(n) - z + NZ, NZ), z).start()
         return carry
 
-    lax.fori_loop(0, NZ - 1, pass_on, 0)
-    pair_sum(NZ - 1, 0)
+    lax.fori_loop(0, NZ - 1, give, 0)
+    deep.stage2()
+    cr[z] = cs[z]
     swap(eo, ei, 0).wait_recv()
-    cr[z] = cs[2 * z + xl]
+    embeds = [emb[2 * z + xl, pl.ds(4 * n, 4)].astype(F32) + er[n, 3, xl].astype(F32) + el[n, 3, xl].astype(F32)
+              + ei[pl.ds(4 * n, 4)].astype(F32) for n in range(2)]
+    xin[...] = jnp.concatenate(embeds, axis=0).reshape(CODEBOOKS * OWN, DD)
 
     def take(k, carry):
         share(k, lax.rem(z + NZ - k, NZ)).wait_recv()
@@ -462,14 +466,15 @@
     def gathered(n, carry):
         context, square = carry
         v = cr[n]
-        return context + v[:, :DD].astype(F32), square + squares(v)
+        hl = v[:, DD:].astype(F32)
+        return context + v[:, :DD].astype(F32), square + hl[:, :1] + hl[:, 64:65]
 
     context, square = lax.fori_loop(0, NZ, gathered, (jnp.zeros((OWN, DD), F32), jnp.zeros((OWN, 1), F32)))
     context = context * lax.rsqrt(square / D + epsilon)
-    embeds = emb[2 * z + xl].astype(F32) + er[3, xl].astype(F32) + el[3, xl].astype(F32) + ei[...].astype(F32)
+    deep.stage3()
 
     rows = CODEBOOKS * OWN
-    x = (context[None] + embeds).reshape(rows, DD)
+    x = (context[None] + xin[...].reshape(CODEBOOKS, OWN, DD)).reshape(rows, DD)
     dn = (x * lax.rsqrt(jnp.mean(x * x, axis=-1, keepdims=True) + epsilon) * dgain[...]).astype(BF16)
     deep.stage4()
 
@@ -504,7 +509,7 @@
         datt[:, cols] = jnp.where(low_half, parts[0], parts[1]).astype(BF16)
         return carry
 
-    lax.fori_loop(0, DHEADS // 2, dattend, 0)
+    lax.fori_loop(0, DHEADS // 2, dattend, 0, unroll=4)
     loads[8].wait()
     out = x + dot(datt[...], wm[...])
     final = (out * lax.rsqrt(jnp.mean(out * out, axis=-1, keepdims=True) + epsilon) * fgain[...]).astype(BF16)
@@ -534,13 +539,13 @@
     shared = OWN * NZ
     lanes = lax.broadcasted_iota(jnp.int32, (shared, 256), 1).astype(F32)
     spots = lax.broadcasted_iota(jnp.int32, (shared, 128), 1)
-    goal = target[...].astype(F32)
-    books = lax.broadcasted_iota(jnp.int32, goal.shape, 1)
+    goals = goal[...].astype(F32) - (z * 256).astype(F32)
+    books = lax.broadcasted_iota(jnp.int32, goals.shape, 1)
 
     def book(c, total):
         logits = dot(fin[c].reshape(shared, DD), wh[c])
         e = jnp.sum(jnp.exp(logits), axis=-1, keepdims=True)
-        want = jnp.sum(jnp.where(books == c, goal, 0.0), axis=1, keepdims=True)
+        want = jnp.sum(jnp.where(books == c, goals, 0.0), axis=1, keepdims=True)
         hit = jnp.sum(jnp.where(lanes == want, logits, 0.0), axis=-1, keepdims=True)
         total = jnp.where(spots == c, e, total)
         return jnp.where(spots == CODEBOOKS + c, hit, total)
@@ -572,7 +577,9 @@
     qkv_flows(lambda f: f.drain())
     mixer.drain()
     deep.drain()
-    ering.drain()
+    erings[0].drain()
+    erings[1].drain()
+    din_x.wait_send()
     pring.drain()
     swap(eo, ei, 0).wait_send()
     swap(po, pi, 1).wait_send()
@@ -581,7 +588,6 @@
 
     def sent(k, carry):
         cross(k).wait_send()
-        over(k).wait_send()
         return carry
 
     def sent_far(k, carry):
@@ -598,17 +604,10 @@
 
 def shards(hidden_in, attn_gain, qkv_weight, mix_weight, out_gain, depth_in_weight, text_table, code_tables,
            depth_gain, depth_qkv, depth_mix, final_gain, heads_weight, text_ids, codes):
-    t = lax.axis_index("tensor")
     half = HEAD_DIM // 2
     angles = np.arange(FRAMES)[:, None] * 10000.0 ** (-np.arange(half) / half)[None, :]
     cosv = np.concatenate([np.cos(angles)] * 2, axis=1).astype(np.float32)
     sinv = np.concatenate([-np.sin(angles), np.sin(angles)], axis=1).astype(np.float32)
-    ids = jnp.concatenate(
-        [text_ids[:, None] - t * text_table.shape[0], codes[:, :CODEBOOKS - 1] - t * code_tables.shape[1]], axis=1)
-    z, xl = t // 2, lax.rem(t, 2)
-    target = lax.dynamic_index_in_dim(codes.reshape(NZ, 2, OWN, CODEBOOKS), xl, 1, keepdims=False)
-    target = target.reshape(NZ * OWN, CODEBOOKS) - z * 256
-
     vmem = pl.BlockSpec(memory_space=pltpu.VMEM)
     anym = pl.BlockSpec(memory_space=pl.ANY)
     dma = pltpu.SemaphoreType.DMA
@@ -621,33 +620,35 @@
         in_specs=[vmem] * 9 + [anym] * 8,
         out_specs=vmem,
         scratch_shapes=[
-            b16(FRAMES, D), b16(256, DD), b16(CODEBOOKS - 1, 128, DD),
+            b16(FRAMES, D), b16(128, 512), b16(2, 256, DD), b16(CODEBOOKS - 1, 128, DD),
+            pltpu.VMEM((128, CODEBOOKS), jnp.int32),
             b16(4, DP, 256, 256), b16(FRAMES, D), f32(3, FRAMES, 256), b16(FRAMES, 256),
             b16(NZ, 3, 128, 256),
             b16(TP, CODEBOOKS, OWN, DD),
-            b16(4, 2, CODEBOOKS, OWN, DD), b16(4, 2, CODEBOOKS, OWN, DD),
+            b16(2, 4, 2, 4, OWN, DD), b16(2, 4, 2, 4, OWN, DD),
             b16(CODEBOOKS, OWN, DD), b16(CODEBOOKS, OWN, DD),
             b16(4, 3, 128, 256), b16(4, 3, 128, 256), b16(128, 256), b16(128, 256),
             b16(NZ, 128, 256), b16(NZ, 128, 256),
-            b16(TP, OWN, wide), b16(NZ, OWN, wide), b16(NZ, OWN, wide),
+            b16(NZ, OWN, wide), b16(NZ, OWN, wide), f32(CODEBOOKS * OWN, DD),
             b16(3, DD, DD), b16(DD, DD), b16(CODEBOOKS, DD, 256),
             b16(3, CODEBOOKS * OWN, DD), b16(CODEBOOKS * OWN, DD),
             b16(CODEBOOKS, NZ, OWN, DD), f32(NZ, OWN, 128), f32(NZ, OWN, 128),
             dma((10,)),
             dma((5, 15)), dma((5, 15)),
-            dma((8,)), dma((8,)),
+            dma((2, 8)), dma((2, 8)),
             dma((8,)), dma((8,)),
             dma((NZ,)), dma((NZ,)),
             dma((2,)), dma((2,)),
-            dma((2, NZ)), dma((2, NZ)),
-            dma((2,)), dma((2,)),
+            dma((NZ,)), dma((NZ,)),
+            dma((3,)), dma((3,)),
             dma((8,)), dma((8,)),
             dma((NZ,)), dma((NZ,)),
         ],
         compiler_params=pltpu.CompilerParams(
             collective_id=0, has_side_effects=True, vmem_limit_bytes=60 * 2**20),
         name="layer",
-    )(attn_gain[None], out_gain[None], text_table, ids, cosv, sinv, depth_gain[None], final_gain[None], target,
+    )(attn_gain[None], out_gain[None], text_table, text_ids.reshape(2, 128), codes, cosv, sinv, depth_gain[None],
+      final_gain[None],
       hidden_in, qkv_weight, mix_weight, depth_in_weight, code_tables, depth_qkv, depth_mix, heads_weight)
 
 

time: 172 us -> 153 us (0.89)
  Pallas kernels: 166 us -> 149 us
  other arithmetic: 2.02 us -> 0 us
    pallas_call x1, Pallas kernels: 166 us -> 149 us  [shards(): pl.pallas_call(layer, out_shape=jax.ShapeDtypeStruct((OWN, CODEBOOKS), F3...]
    sub x3 -> x0, other arithmetic: 2.01 us -> none  [the longest x1 0.7 us: shards(): codes[:, :CODEBOOKS - 1] - t * code_tables.shape[1]]
where the time goes in v3:
time: 153 us; the launch traced here: 152 us
  Pallas kernels  149 us (97%)
  local copies, waits for them, and re-layouts  2.82 us (2%)
    pallas_call x1, Pallas kernels, shards(): pl.pallas_call(layer, out_shape=jax.ShapeDtypeStruct((OWN, CODEBOOKS), F3...  149 us

profile of v3, /device:TPU:4, one launch (start us, length us, event | category | flops | bytes accessed | tf_op | source)
XLA Modules:
  0.0 152.3 jit_solution(17502014094175866101)
XLA Ops:
  0.0 1.5 copy.18.code
  1.5 149.5 %layer.1 = f32[16,8]{1,0:T(8,128)} custom-call(f32[1,4096]{1,0:T(1,128)} %bitcast.5, f32[1,4096]{1,0:T(1,128)} %bitcast.6, bf16[1000,1024]{1,0:T(8,128)(2,1)} %text.1, s32[2,128]{1,0:T(2,128)} %bitcast.9, s32[256,8]{1,0:T(8,128)} %copy.18.code, f32[256,128]{1,0:T(8,128)} %constant.4.clone.cosr, f32[256,128]{1,0:T(8,128)} %constant.5.clone.sinr, ...), custom_call_target="tpu_custom_call" | custom-call | tf_op jit(solution)/shard_map/layer/pallas_call | solution.py:617
  151.0 1.4 copy.19

commit v4 on v3

--- a/solution.py
+++ b/solution.py
@@ -127,34 +127,93 @@
             self.copy(kind, p.d, p.cpeer).wait_send()
 
 
+class FlowDeep(Flow):
+    def start0(self):
+        p = self.pos
+        pltpu.make_async_remote_copy(
+            src_ref=self.own, dst_ref=self.block(p.d), send_sem=self.ss(X0), recv_sem=self.rs(X0),
+            device_id={"dp": p.xpeer, "tensor": p.xsib}, device_id_type=MESH).start()
+        for kind, dev in ((R1, p.up), (L1, p.down), (C0, p.cpeer)):
+            self.copy(kind, p.d, dev, own=True).start()
+
+
+class FlowY(Flow):
+    def half(self, kind, idx, dev, which):
+        view = self.block(idx).at[pl.ds(which * 128, 128)]
+        return pltpu.make_async_remote_copy(
+            src_ref=view, dst_ref=view, send_sem=self.ss(kind), recv_sem=self.rs(kind),
+            device_id={"dp": dev}, device_id_type=MESH)
+
+    def start0(self):
+        p = self.pos
+        for kind, dev in ((R1, p.up), (L1, p.down), (X0, p.xpeer), (C0, p.cpeer)):
+            self.copy(kind, p.d, dev, own=True).start()
+
+    def across(self, kind, idx):
+        self.forward(kind, idx, self.pos.xpeer)
+
+    def stage1(self):
+        p = self.pos
+        self.got(R1)
+        self.half(L3, p.down, p.up, 0).start()
+        self.across(R2, p.down)
+        self.forward(C0 + 2, p.down, p.cpeer)
+        self.got(L1)
+        self.half(15, p.up, p.down, 1).start()
+        self.across(L2, p.up)
+        self.forward(C0 + 3, p.up, p.cpeer)
+        self.got(X0)
+        self.forward(C0 + 1, p.xpeer, p.cpeer)
+
+    def stage2(self):
+        p = self.pos
+        self.half(L3, p.far, p.up, 0).wait_recv()
+        self.half(15, p.far, p.down, 1).wait_recv()
+        self.across(R3, p.far)
+        self.forward(C0 + 6, p.far, p.cpeer)
+        self.got(R2)
+        self.forward(C0 + 4, p.blocks[4], p.cpeer)
+        self.got(L2)
+        self.forward(C0 + 5, p.blocks[5], p.cpeer)
+
+    def stage3(self):
+        p = self.pos
+        self.got(R3)
+        self.forward(C0 + 7, p.blocks[7], p.cpeer)
+
+    def drain(self):
+        p = self.pos
+        for kind in range(16):
+            if kind in (L3, 15):
+                self.half(kind, p.d, p.up, 0).wait_send()
+            else:
+                self.copy(kind, p.d, p.cpeer).wait_send()
+
+
 class Ring:
-    def __init__(self, pos, own, slots, half, add, ss, rs):
-        self.pos, self.own, self.slots, self.half, self.add = pos, own, slots, half, add
+    def __init__(self, pos, own, slots, long, add, ss, rs):
+        self.pos, self.own, self.slots, self.long, self.add = pos, own, slots, long, add
         self.ss, self.rs = ss, rs
+
+    def first(self, way):
+        return 0 if way == self.long else 1
 
     def dest(self, way, s):
         return lax.rem(self.pos.z + (4 - s if way == 0 else 4 + s), NZ)
 
     def copy(self, way, s):
         slots = self.slots[way]
-        if s == 0:
-            part = pl.ds(way * self.half, self.half)
-            src, dst = self.own(self.dest(way, 0)).at[:, part], slots.at[0, :, part]
-        else:
-            src, dst = slots.at[s - 1], slots.at[s]
+        src = self.own(self.dest(way, s)) if s == self.first(way) else slots.at[s - 1]
         k = 4 * way + s
         return pltpu.make_async_remote_copy(
-            src_ref=src, dst_ref=dst, send_sem=self.ss.at[k], recv_sem=self.rs.at[k],
+            src_ref=src, dst_ref=slots.at[s], send_sem=self.ss.at[k], recv_sem=self.rs.at[k],
             device_id={"tensor": self.pos.zdown if way else self.pos.zup}, device_id_type=MESH)
-
-    def clear(self):
-        for way in range(2):
-            rest = pl.ds((1 - way) * self.half, self.half)
-            self.slots[way][0, :, rest] = jnp.zeros_like(self.slots[way][0, :, rest])
 
     def step(self, s):
         for way in range(2):
-            if s:
+            if s < self.first(way):
+                continue
+            if s > self.first(way):
                 self.copy(way, s - 1).wait_recv()
                 self.add(self.slots[way].at[s - 1], self.own(self.dest(way, s)))
             self.copy(way, s).start()
@@ -165,15 +224,15 @@
 
     def drain(self):
         for way in range(2):
-            for s in range(4):
+            for s in range(self.first(way), 4):
                 self.copy(way, s).wait_send()
 
 
-def layer(gain, ogain, text, tid, code, cosr, sinr, dgain, fgain,
-          hid_h, qkv_h, mix_h, din_h, tabs_h, dqkv, dmix_h, heads,
+def layer(gain, ogain, tid, code, cosr, sinr, dgain, fgain,
+          hid_h, text_h, qkv_h, mix_h, din_h, tabs_h, dqkv, dmix_h, heads,
           loss,
-          hid, hown, din, tabs, goal, wall, normed, acc, att, part, emb, er, el, eo, ei, pr, pe, po, pi, bs, br,
-          cs, cr, xin, wq, wm, wh, proj, datt, fin, sums, got,
+          hid, text, hown, din, tabs, goal, wall, normed, acc, att, part, emb, er, el, eo, ei, pr, pe, po, pi, bs, br,
+          cs, cr, xin, wq, wm, wh, hx, proj, datt, fin, sums, got,
           lsem, wss, wrs, ess, ers, pss, prs, bss, brs, xss, xrs, css, crs, hss, hrs, fss, frs, tss, trs):
     p = Places()
     d, t, z, xl = p.d, p.t, p.z, p.xl
@@ -186,7 +245,7 @@
     sib_lanes = pl.ds(pl.multiple_of((1 - xl) * 128, 128), 128)
     loads = [(qkv_h.at[0], wall.at[0, d]), (qkv_h.at[1], wall.at[1, d]), (qkv_h.at[2], wall.at[2, d]),
              (mix_h, wall.at[3, d]), (tabs_h, tabs), (hid_h, hid), (din_h, din.at[xl]), (dqkv, deep_block(d)),
-             (dmix_h, wm), (heads, wh.at[:, :, own_lanes])]
+             (dmix_h, wm), (heads, wh.at[:, :, own_lanes]), (text_h, text)]
     loads = [pltpu.make_async_copy(src, dst, lsem.at[n]) for n, (src, dst) in enumerate(loads)]
     for one in loads:
         one.start()
@@ -208,13 +267,15 @@
 
     def ering_of(n):
         books = pl.ds(4 * n, 4)
-        return Ring(p, lambda i: emb.at[pl.ds(2 * i, 2), books], (er.at[n], el.at[n]), 2, add_books, ess.at[n], ers.at[n])
+        return Ring(p, lambda i: emb.at[pl.ds(2 * i, 2), books], (er.at[n], el.at[n]), n, add_books, ess.at[n], ers.at[n])
 
     erings = [ering_of(n) for n in range(2)]
-    pring = Ring(p, lambda i: part.at[i], (pr, pe), 64, add_rows, pss, prs)
-    erings[0].clear()
-    erings[1].clear()
-    pring.clear()
+
+    def pring_of(n):
+        rows = pl.ds(64 * n, 64)
+        return Ring(p, lambda i: part.at[i, :, rows], (pr.at[n], pe.at[n]), n, add_rows, pss.at[n], prs.at[n])
+
+    prings = [pring_of(n) for n in range(2)]
 
     barrier = pltpu.get_barrier_semaphore()
     for dev in (p.xpeer, p.up, p.down, p.cpeer):
@@ -226,23 +287,19 @@
 
     lax.fori_loop(1, NZ, greet, 0)
     pl.semaphore_signal(barrier, inc=1, device_id={"tensor": p.xsib}, device_id_type=MESH)
-    pl.semaphore_wait(barrier, 4 + NZ)
+    pl.semaphore_signal(barrier, inc=1, device_id={"dp": p.xpeer, "tensor": p.xsib}, device_id_type=MESH)
+    pl.semaphore_wait(barrier, 5 + NZ)
 
     def flow(f):
-        return Flow(p, wall.at[f, d], block_of(f), lambda k: wss.at[f, k], lambda k: wrs.at[f, k])
-
-    def qkv_flows(act):
-        def one(f, carry):
-            act(flow(f))
-            return carry
-
-        lax.fori_loop(0, 3, one, 0)
+        kind = FlowY if f == 2 else Flow
+        return kind(p, wall.at[f, d], block_of(f), lambda k: wss.at[f, k], lambda k: wrs.at[f, k])
 
     mixer = flow(3)
-    deep = Flow(p, dqkv, deep_block, lambda k: wss.at[4, k], lambda k: wrs.at[4, k])
+    deep = FlowDeep(p, dqkv, deep_block, lambda k: wss.at[4, k], lambda k: wrs.at[4, k])
     for n in range(3):
         loads[n].wait()
-    qkv_flows(lambda f: f.start0())
+    for f in range(3):
+        flow(f).start0()
 
     codev = code[...].astype(F32)
     pick = lax.broadcasted_iota(jnp.int32, codev.shape, 1)
@@ -258,6 +315,7 @@
         lanes = lax.broadcasted_iota(jnp.int32, (FRAMES, width), 1).astype(F32) + start
         return (lanes == want).astype(BF16)
 
+    loads[10].wait()
     found = dot(named(text_want, 0, whole), text[:whole])
     if count > whole:
         found = found + dot(named(text_want, whole, count - whole), text[whole:])
@@ -304,7 +362,7 @@
             acc[i] = got_one if first else acc[i] + got_one
             return carry
 
-        lax.fori_loop(0, 3, one, 0)
+        lax.fori_loop(0, 3, one, 0, unroll=3)
 
     flow(0).stage1()
     erings[0].step(1)
@@ -313,15 +371,6 @@
     flow(2).stage1()
     loads[3].wait()
     mixer.start0()
-    din_x = pltpu.make_async_remote_copy(
-        src_ref=din_h, dst_ref=din.at[xl], send_sem=hss.at[2], recv_sem=hrs.at[2],
-        device_id={"tensor": p.xsib}, device_id_type=MESH)
-    din_x.start()
-    head_part = pl.ds(p.core * 4, 4)
-    head_rest = pl.ds(4 - p.core * 4, 4)
-    head_x = pltpu.make_async_remote_copy(
-        src_ref=heads.at[head_part], dst_ref=wh.at[head_part, :, own_lanes], send_sem=hss.at[0],
-        recv_sem=hrs.at[0], device_id={"tensor": p.xsib}, device_id_type=MESH)
     project((0, 1), True)
     flow(0).stage2()
     erings[0].step(2)
@@ -330,12 +379,25 @@
     mixer.stage1()
     erings[1].step(2)
     project((2, 4))
-    project((3, 5))
     for f in range(3):
         flow(f).stage3()
     mixer.stage2()
     loads[7].wait()
     deep.start0()
+    din_part = pl.ds(pl.multiple_of(128 * p.core, 128), 128)
+    din_rest = pl.ds(pl.multiple_of(128 - 128 * p.core, 128), 128)
+    din_x = pltpu.make_async_remote_copy(
+        src_ref=din_h.at[din_part], dst_ref=din.at[xl, din_part], send_sem=hss.at[2], recv_sem=hrs.at[2],
+        device_id={"tensor": p.xsib}, device_id_type=MESH)
+    din_x.start()
+
+    def din_core(some):
+        view = din.at[1 - xl, some]
+        return pltpu.make_async_remote_copy(
+            src_ref=view, dst_ref=view, send_sem=hss.at[3], recv_sem=hrs.at[3],
+            device_id={"dp": p.cpeer}, device_id_type=MESH)
+
+    project((3, 5))
     erings[0].step(3)
     project((6, 7))
 
@@ -361,7 +423,7 @@
             att[side * 128:side * 128 + 128, cols] = mixed_rows[:, side].reshape(128, HEAD_DIM)
         return carry
 
-    lax.fori_loop(0, 2, attend, 0)
+    lax.fori_loop(0, 2, attend, 0, unroll=2)
     erings[1].step(3)
     mixer.stage3()
     mixer.stage4()
@@ -386,8 +448,7 @@
         part[zz, 1] = one[128:]
         return carry
 
-    lax.fori_loop(0, NZ, mixed, 0)
-    head_x.start()
+    lax.fori_loop(0, NZ, mixed, 0, unroll=2)
 
     def crossed(n, carry):
         zz = near_far(n)
@@ -396,10 +457,15 @@
         return carry
 
     crossed(0, 0)
-    pring.step(0)
+    for n in range(2):
+        prings[n].step(0)
     lax.fori_loop(1, NZ, crossed, 0)
-    pring.step(1)
-    pring.step(2)
+    for n in range(2):
+        prings[n].step(1)
+    din_x.wait_recv()
+    din_core(din_part).start()
+    for n in range(2):
+        prings[n].step(2)
     deep.stage1()
 
     def swap(src, dst, k):
@@ -407,21 +473,32 @@
             src_ref=src, dst_ref=dst, send_sem=xss.at[k], recv_sem=xrs.at[k],
             device_id={"tensor": p.xsib}, device_id_type=MESH)
 
-    pring.step(3)
+    for n in range(2):
+        prings[n].step(3)
+    deep.stage2()
     for n in range(2):
         erings[n].arrive()
         mine = pl.ds(4 * n, 4)
         eo[mine] = emb[2 * z + 1 - xl, mine] + er[n, 3, 1 - xl] + el[n, 3, 1 - xl]
     swap(eo, ei, 0).start()
-    pring.arrive()
+    for n in range(2):
+        prings[n].arrive()
 
     def total(h):
-        return part[z, h].astype(F32) + pr[3, h].astype(F32) + pe[3, h].astype(F32)
+        sides = [pr[n, 3, h].astype(F32) + pe[n, 3, h].astype(F32) for n in range(2)]
+        return part[z, h].astype(F32) + jnp.concatenate(sides, axis=0)
 
     po[...] = total(1 - xl).astype(BF16)
     swap(po, pi, 1).start()
+    head_part = pl.ds(p.core * 4, 4)
+    head_rest = pl.ds(4 - p.core * 4, 4)
+    head_x = pltpu.make_async_remote_copy(
+        src_ref=heads.at[head_part], dst_ref=hx.at[head_part], send_sem=hss.at[0],
+        recv_sem=hrs.at[0], device_id={"tensor": p.xsib}, device_id_type=MESH)
+    head_x.start()
+    deep.stage3()
     loads[6].wait()
-    din_x.wait_recv()
+    din_core(din_rest).wait_recv()
 
     def scale_cols(b, summed):
         resid = summed + hown[:, b * 256:b * 256 + 256].astype(F32)
@@ -450,7 +527,6 @@
         return carry
 
     lax.fori_loop(0, NZ - 1, give, 0)
-    deep.stage2()
     cr[z] = cs[z]
     swap(eo, ei, 0).wait_recv()
     embeds = [emb[2 * z + xl, pl.ds(4 * n, 4)].astype(F32) + er[n, 3, xl].astype(F32) + el[n, 3, xl].astype(F32)
@@ -471,7 +547,6 @@
 
     context, square = lax.fori_loop(0, NZ, gathered, (jnp.zeros((OWN, DD), F32), jnp.zeros((OWN, 1), F32)))
     context = context * lax.rsqrt(square / D + epsilon)
-    deep.stage3()
 
     rows = CODEBOOKS * OWN
     x = (context[None] + xin[...].reshape(CODEBOOKS, OWN, DD)).reshape(rows, DD)
@@ -482,15 +557,7 @@
         proj[i] = dot(dn, wq[i]).astype(BF16)
         return carry
 
-    lax.fori_loop(0, 3, dproject, 0)
-    head_x_in = pltpu.make_async_remote_copy(
-        src_ref=wh.at[head_part, :, sib_lanes], dst_ref=wh.at[head_part, :, sib_lanes], send_sem=hss.at[1],
-        recv_sem=hrs.at[0], device_id={"dp": p.cpeer}, device_id_type=MESH)
-    head_x_in.wait_recv()
-    head_c = pltpu.make_async_remote_copy(
-        src_ref=wh.at[head_part, :, sib_lanes], dst_ref=wh.at[head_part, :, sib_lanes], send_sem=hss.at[1],
-        recv_sem=hrs.at[1], device_id={"dp": p.cpeer}, device_id_type=MESH)
-    head_c.start()
+    lax.fori_loop(0, 3, dproject, 0, unroll=3)
 
     rq = lax.broadcasted_iota(jnp.int32, (rows, rows), 0)
     rk = lax.broadcasted_iota(jnp.int32, (rows, rows), 1)
@@ -515,27 +582,45 @@
     final = (out * lax.rsqrt(jnp.mean(out * out, axis=-1, keepdims=True) + epsilon) * fgain[...]).astype(BF16)
     fin[:, z] = final.reshape(CODEBOOKS, OWN, DD)
 
-    def ring(way, s, block):
-        books = pl.ds(0, CODEBOOKS) if s < 3 else pl.ds(4 * way, 4)
-        view = fin.at[books, block]
-        return pltpu.make_async_remote_copy(
-            src_ref=view, dst_ref=view, send_sem=fss.at[4 * way + s], recv_sem=frs.at[4 * way + s],
+    head_x_in = pltpu.make_async_remote_copy(
+        src_ref=hx.at[head_part], dst_ref=hx.at[head_part], send_sem=hss.at[1],
+        recv_sem=hrs.at[0], device_id={"dp": p.cpeer}, device_id_type=MESH)
+    head_c = pltpu.make_async_remote_copy(
+        src_ref=hx.at[head_part], dst_ref=hx.at[head_part], send_sem=hss.at[1],
+        recv_sem=hrs.at[1], device_id={"dp": p.cpeer}, device_id_type=MESH)
+    head_c_in = pltpu.make_async_remote_copy(
+        src_ref=hx.at[head_rest], dst_ref=hx.at[head_rest], send_sem=hss.at[1],
+        recv_sem=hrs.at[1], device_id={"dp": p.cpeer}, device_id_type=MESH)
+    placed = [pltpu.make_async_copy(hx.at[some], wh.at[some, :, sib_lanes], lsem.at[11 + n])
+              for n, some in enumerate((head_part, head_rest))]
+
+    def ring(n, way, s, block):
+        view = fin.at[pl.ds(4 * n, 4), block]
+        return pltpu.make_async_remote_copy(
+            src_ref=view, dst_ref=view, send_sem=fss.at[n, 4 * way + s], recv_sem=frs.at[n, 4 * way + s],
             device_id={"tensor": p.zdown if way else p.zup}, device_id_type=MESH)
 
     for s in range(4):
-        for way in range(2):
-            block = lax.rem(z + (s if way else NZ - s), NZ)
-            if s:
-                ring(way, s - 1, block).wait_recv()
-            ring(way, s, block).start()
-    far = lax.rem(z + 4, NZ)
-    ring(0, 3, far).wait_recv()
-    ring(1, 3, far).wait_recv()
+        for n in range(2):
+            for way in range(2):
+                block = lax.rem(z + (s if way else NZ - s), NZ)
+                if s:
+                    ring(n, way, s - 1, block).wait_recv()
+                if s < 3 or way == n:
+                    ring(n, way, s, block).start()
+        if s == 2:
+            head_x_in.wait_recv()
+            head_c.start()
+            placed[0].start()
+        if s == 3:
+            head_c_in.wait_recv()
+            placed[1].start()
+    for n in range(2):
+        ring(n, n, 3, lax.rem(z + 4, NZ)).wait_recv()
 
     loads[9].wait()
-    pltpu.make_async_remote_copy(
-        src_ref=wh.at[head_rest, :, sib_lanes], dst_ref=wh.at[head_rest, :, sib_lanes], send_sem=hss.at[1],
-        recv_sem=hrs.at[1], device_id={"dp": p.cpeer}, device_id_type=MESH).wait_recv()
+    placed[0].wait()
+    placed[1].wait()
     shared = OWN * NZ
     lanes = lax.broadcasted_iota(jnp.int32, (shared, 256), 1).astype(F32)
     spots = lax.broadcasted_iota(jnp.int32, (shared, 128), 1)
@@ -550,7 +635,7 @@
         total = jnp.where(spots == c, e, total)
         return jnp.where(spots == CODEBOOKS + c, hit, total)
 
-    sums[...] = lax.fori_loop(0, CODEBOOKS, book, jnp.zeros((shared, 128), F32)).reshape(NZ, OWN, 128)
+    sums[...] = lax.fori_loop(0, CODEBOOKS, book, jnp.zeros((shared, 128), F32), unroll=4).reshape(NZ, OWN, 128)
 
     def reply(k, sender):
         to = lax.rem(z + k, NZ)
@@ -574,13 +659,16 @@
         both = both + got[n]
     loss[...] = jnp.log(both[:, :CODEBOOKS]) - both[:, CODEBOOKS:2 * CODEBOOKS]
 
-    qkv_flows(lambda f: f.drain())
+    for f in range(3):
+        flow(f).drain()
     mixer.drain()
     deep.drain()
     erings[0].drain()
     erings[1].drain()
     din_x.wait_send()
-    pring.drain()
+    din_core(din_part).wait_send()
+    prings[0].drain()
+    prings[1].drain()
     swap(eo, ei, 0).wait_send()
     swap(po, pi, 1).wait_send()
     head_x.wait_send()
@@ -597,9 +685,10 @@
 
     lax.fori_loop(0, NZ, sent, 0)
     lax.fori_loop(1, NZ, sent_far, 0)
-    for s in range(4):
+    for n in range(2):
         for way in range(2):
-            ring(way, s, z).wait_send()
+            for s in range(4 if way == n else 3):
+                ring(n, way, s, z).wait_send()
 
 
 def shards(hidden_in, attn_gain, qkv_weight, mix_weight, out_gain, depth_in_weight, text_table, code_tables,
@@ -617,39 +706,39 @@
     return pl.pallas_call(
         layer,
         out_shape=jax.ShapeDtypeStruct((OWN, CODEBOOKS), F32),
-        in_specs=[vmem] * 9 + [anym] * 8,
+        in_specs=[vmem] * 8 + [anym] * 9,
         out_specs=vmem,
         scratch_shapes=[
-            b16(FRAMES, D), b16(128, 512), b16(2, 256, DD), b16(CODEBOOKS - 1, 128, DD),
+            b16(FRAMES, D), b16(*text_table.shape), b16(128, 512), b16(2, 256, DD), b16(CODEBOOKS - 1, 128, DD),
             pltpu.VMEM((128, CODEBOOKS), jnp.int32),
             b16(4, DP, 256, 256), b16(FRAMES, D), f32(3, FRAMES, 256), b16(FRAMES, 256),
             b16(NZ, 3, 128, 256),
             b16(TP, CODEBOOKS, OWN, DD),
             b16(2, 4, 2, 4, OWN, DD), b16(2, 4, 2, 4, OWN, DD),
             b16(CODEBOOKS, OWN, DD), b16(CODEBOOKS, OWN, DD),
-            b16(4, 3, 128, 256), b16(4, 3, 128, 256), b16(128, 256), b16(128, 256),
+            b16(2, 4, 3, 64, 256), b16(2, 4, 3, 64, 256), b16(128, 256), b16(128, 256),
             b16(NZ, 128, 256), b16(NZ, 128, 256),
             b16(NZ, OWN, wide), b16(NZ, OWN, wide), f32(CODEBOOKS * OWN, DD),
-            b16(3, DD, DD), b16(DD, DD), b16(CODEBOOKS, DD, 256),
+            b16(3, DD, DD), b16(DD, DD), b16(CODEBOOKS, DD, 256), b16(CODEBOOKS, DD, 128),
             b16(3, CODEBOOKS * OWN, DD), b16(CODEBOOKS * OWN, DD),
             b16(CODEBOOKS, NZ, OWN, DD), f32(NZ, OWN, 128), f32(NZ, OWN, 128),
-            dma((10,)),
-            dma((5, 15)), dma((5, 15)),
+            dma((13,)),
+            dma((5, 16)), dma((5, 16)),
             dma((2, 8)), dma((2, 8)),
-            dma((8,)), dma((8,)),
+            dma((2, 8)), dma((2, 8)),
             dma((NZ,)), dma((NZ,)),
             dma((2,)), dma((2,)),
             dma((NZ,)), dma((NZ,)),
-            dma((3,)), dma((3,)),
-            dma((8,)), dma((8,)),
+            dma((4,)), dma((4,)),
+            dma((2, 8)), dma((2, 8)),
             dma((NZ,)), dma((NZ,)),
         ],
         compiler_params=pltpu.CompilerParams(
             collective_id=0, has_side_effects=True, vmem_limit_bytes=60 * 2**20),
         name="layer",
-    )(attn_gain[None], out_gain[None], text_table, text_ids.reshape(2, 128), codes, cosv, sinv, depth_gain[None],
+    )(attn_gain[None], out_gain[None], text_ids.reshape(2, 128), codes, cosv, sinv, depth_gain[None],
       final_gain[None],
-      hidden_in, qkv_weight, mix_weight, depth_in_weight, code_tables, depth_qkv, depth_mix, heads_weight)
+      hidden_in, text_table, qkv_weight, mix_weight, depth_in_weight, code_tables, depth_qkv, depth_mix, heads_weight)
 
 
 def solution(mesh):

time: 153 us -> 138 us (0.902)
  Pallas kernels: 149 us -> 135 us
    pallas_call x1, Pallas kernels: 149 us -> 135 us  [shards(): pl.pallas_call(layer, out_shape=jax.ShapeDtypeStruct((OWN, CODEBOOKS), F3...]
where the time goes in v4:
time: 138 us
  Pallas kernels  135 us (98%)
  local copies, waits for them, and re-layouts  2.82 us (2%)
    pallas_call x1, Pallas kernels, shards(): pl.pallas_call(layer, out_shape=jax.ShapeDtypeStruct((OWN, CODEBOOKS), F3...  135 us

profile of v4, /device:TPU:4, one launch (start us, length us, event | category | flops | bytes accessed | tf_op | source)
XLA Modules:
  0.0 137.8 jit_solution(14705738600375869078)
XLA Ops:
  0.0 1.5 %copy.18.code = s32[256,8]{1,0:T(8,128)} copy(s32[256,8]{0,1:T(8,128)} %param.31) | data formatting | bytes 16384 | tf_op args[14]
  1.5 135.0 %layer.1 = f32[16,8]{1,0:T(8,128)} custom-call(f32[1,4096]{1,0:T(1,128)} %bitcast.5, f32[1,4096]{1,0:T(1,128)} %bitcast.6, s32[2,128]{1,0:T(2,128)} %bitcast.9, s32[256,8]{1,0:T(8,128)} %copy.18.code, f32[256,128]{1,0:T(8,128)} %constant.4.clone.cosr, f32[256,128]{1,0:T(8,128)} %constant.5.clone.sinr, f32[1,1024]{1,0:T(1,128)} %bitcast.7, ...), custom_call_target="tpu_custom_call" | custom-call | tf_op jit(solution)/shard_map/layer/pallas_call | solution.py:706
  136.4 1.4 copy.19

commit v5 on v4

--- a/solution.py
+++ b/solution.py
@@ -459,23 +459,24 @@
     crossed(0, 0)
     for n in range(2):
         prings[n].step(0)
-    lax.fori_loop(1, NZ, crossed, 0)
+    lax.fori_loop(1, 3, crossed, 0)
     for n in range(2):
         prings[n].step(1)
     din_x.wait_recv()
     din_core(din_part).start()
+    lax.fori_loop(3, 5, crossed, 0)
     for n in range(2):
         prings[n].step(2)
-    deep.stage1()
 
     def swap(src, dst, k):
         return pltpu.make_async_remote_copy(
             src_ref=src, dst_ref=dst, send_sem=xss.at[k], recv_sem=xrs.at[k],
             device_id={"tensor": p.xsib}, device_id_type=MESH)
 
+    lax.fori_loop(5, 7, crossed, 0)
     for n in range(2):
         prings[n].step(3)
-    deep.stage2()
+    deep.stage1()
     for n in range(2):
         erings[n].arrive()
         mine = pl.ds(4 * n, 4)
@@ -483,6 +484,8 @@
     swap(eo, ei, 0).start()
     for n in range(2):
         prings[n].arrive()
+
+    crossed(7, 0)
 
     def total(h):
         sides = [pr[n, 3, h].astype(F32) + pe[n, 3, h].astype(F32) for n in range(2)]
@@ -496,7 +499,7 @@
         src_ref=heads.at[head_part], dst_ref=hx.at[head_part], send_sem=hss.at[0],
         recv_sem=hrs.at[0], device_id={"tensor": p.xsib}, device_id_type=MESH)
     head_x.start()
-    deep.stage3()
+    deep.stage2()
     loads[6].wait()
     din_core(din_rest).wait_recv()
 
@@ -527,6 +530,7 @@
         return carry
 
     lax.fori_loop(0, NZ - 1, give, 0)
+    deep.stage3()
     cr[z] = cs[z]
     swap(eo, ei, 0).wait_recv()
     embeds = [emb[2 * z + xl, pl.ds(4 * n, 4)].astype(F32) + er[n, 3, xl].astype(F32) + el[n, 3, xl].astype(F32)
@@ -547,6 +551,12 @@
 
     context, square = lax.fori_loop(0, NZ, gathered, (jnp.zeros((OWN, DD), F32), jnp.zeros((OWN, 1), F32)))
     context = context * lax.rsqrt(square / D + epsilon)
+
+    def ring(n, way, s, block):
+        view = fin.at[pl.ds(2 * n, 2), block]
+        return pltpu.make_async_remote_copy(
+            src_ref=view, dst_ref=view, send_sem=fss.at[n, 4 * way + s], recv_sem=frs.at[n, 4 * way + s],
+            device_id={"tensor": p.zdown if way else p.zup}, device_id_type=MESH)
 
     rows = CODEBOOKS * OWN
     x = (context[None] + xin[...].reshape(CODEBOOKS, OWN, DD)).reshape(rows, DD)
@@ -581,6 +591,10 @@
     out = x + dot(datt[...], wm[...])
     final = (out * lax.rsqrt(jnp.mean(out * out, axis=-1, keepdims=True) + epsilon) * fgain[...]).astype(BF16)
     fin[:, z] = final.reshape(CODEBOOKS, OWN, DD)
+
+    for n in range(4):
+        for way in range(2):
+            ring(n, way, 0, z).start()
 
     head_x_in = pltpu.make_async_remote_copy(
         src_ref=hx.at[head_part], dst_ref=hx.at[head_part], send_sem=hss.at[1],
@@ -594,20 +608,31 @@
     placed = [pltpu.make_async_copy(hx.at[some], wh.at[some, :, sib_lanes], lsem.at[11 + n])
               for n, some in enumerate((head_part, head_rest))]
 
-    def ring(n, way, s, block):
-        view = fin.at[pl.ds(4 * n, 4), block]
-        return pltpu.make_async_remote_copy(
-            src_ref=view, dst_ref=view, send_sem=fss.at[n, 4 * way + s], recv_sem=frs.at[n, 4 * way + s],
-            device_id={"tensor": p.zdown if way else p.zup}, device_id_type=MESH)
-
-    for s in range(4):
-        for n in range(2):
+    for s in range(1, 4):
+        for n in range(4):
             for way in range(2):
                 block = lax.rem(z + (s if way else NZ - s), NZ)
-                if s:
-                    ring(n, way, s - 1, block).wait_recv()
-                if s < 3 or way == n:
+                ring(n, way, s - 1, block).wait_recv()
+                if s < 3 or way == n % 2:
                     ring(n, way, s, block).start()
+        if s == 1:
+            for one in (flow(0), flow(1), flow(2), mixer, deep, erings[0], erings[1], prings[0], prings[1]):
+                one.drain()
+            din_x.wait_send()
+            din_core(din_part).wait_send()
+            swap(eo, ei, 0).wait_send()
+            swap(po, pi, 1).wait_send()
+
+            def sent(k, carry):
+                cross(k).wait_send()
+                return carry
+
+            def sent_far(k, carry):
+                share(k, z).wait_send()
+                return carry
+
+            lax.fori_loop(0, NZ, sent, 0)
+            lax.fori_loop(1, NZ, sent_far, 0)
         if s == 2:
             head_x_in.wait_recv()
             head_c.start()
@@ -615,8 +640,6 @@
         if s == 3:
             head_c_in.wait_recv()
             placed[1].start()
-    for n in range(2):
-        ring(n, n, 3, lax.rem(z + 4, NZ)).wait_recv()
 
     loads[9].wait()
     placed[0].wait()
@@ -635,7 +658,12 @@
         total = jnp.where(spots == c, e, total)
         return jnp.where(spots == CODEBOOKS + c, hit, total)
 
-    sums[...] = lax.fori_loop(0, CODEBOOKS, book, jnp.zeros((shared, 128), F32), unroll=4).reshape(NZ, OWN, 128)
+    total_sums = jnp.zeros((shared, 128), F32)
+    for h in range(2):
+        for n in range(2 * h, 2 * h + 2):
+            ring(n, n % 2, 3, lax.rem(z + 4, NZ)).wait_recv()
+        total_sums = lax.fori_loop(4 * h, 4 * h + 4, book, total_sums, unroll=4)
+    sums[...] = total_sums.reshape(NZ, OWN, 128)
 
     def reply(k, sender):
         to = lax.rem(z + k, NZ)
@@ -659,35 +687,17 @@
         both = both + got[n]
     loss[...] = jnp.log(both[:, :CODEBOOKS]) - both[:, CODEBOOKS:2 * CODEBOOKS]
 
-    for f in range(3):
-        flow(f).drain()
-    mixer.drain()
-    deep.drain()
-    erings[0].drain()
-    erings[1].drain()
-    din_x.wait_send()
-    din_core(din_part).wait_send()
-    prings[0].drain()
-    prings[1].drain()
-    swap(eo, ei, 0).wait_send()
-    swap(po, pi, 1).wait_send()
     head_x.wait_send()
     head_c.wait_send()
 
-    def sent(k, carry):
-        cross(k).wait_send()
-        return carry
-
-    def sent_far(k, carry):
-        share(k, z).wait_send()
+    def reply_sent(k, carry):
         reply(k, z).wait_send()
         return carry
 
-    lax.fori_loop(0, NZ, sent, 0)
-    lax.fori_loop(1, NZ, sent_far, 0)
-    for n in range(2):
+    lax.fori_loop(1, NZ, reply_sent, 0)
+    for n in range(4):
         for way in range(2):
-            for s in range(4 if way == n else 3):
+            for s in range(4 if way == n % 2 else 3):
                 ring(n, way, s, z).wait_send()
 
 
@@ -730,7 +740,7 @@
             dma((2,)), dma((2,)),
             dma((NZ,)), dma((NZ,)),
             dma((4,)), dma((4,)),
-            dma((2, 8)), dma((2, 8)),
+            dma((4, 8)), dma((4, 8)),
             dma((NZ,)), dma((NZ,)),
         ],
         compiler_params=pltpu.CompilerParams(

time: 138 us -> 129 us (0.935)
  Pallas kernels: 135 us -> 126 us
    pallas_call x1, Pallas kernels: 135 us -> 126 us  [shards(): pl.pallas_call(layer, out_shape=jax.ShapeDtypeStruct((OWN, CODEBOOKS), F3...]
where the time goes in v5:
time: 129 us
  Pallas kernels  126 us (98%)
  local copies, waits for them, and re-layouts  2.82 us (2%)
    pallas_call x1, Pallas kernels, shards(): pl.pallas_call(layer, out_shape=jax.ShapeDtypeStruct((OWN, CODEBOOKS), F3...  126 us

profile of v5, /device:TPU:4, one launch (start us, length us, event | category | flops | bytes accessed | tf_op | source)
XLA Modules:
  0.0 128.6 jit_solution(2843823122269510601)
XLA Ops:
  0.0 1.5 %copy.18.code = s32[256,8]{1,0:T(8,128)} copy(s32[256,8]{0,1:T(8,128)} %param.31) | data formatting | bytes 16384 | tf_op args[14]
  1.5 125.7 %layer.1 = f32[16,8]{1,0:T(8,128)} custom-call(f32[1,4096]{1,0:T(1,128)} %bitcast.5, f32[1,4096]{1,0:T(1,128)} %bitcast.6, s32[2,128]{1,0:T(2,128)} %bitcast.9, s32[256,8]{1,0:T(8,128)} %copy.18.code, f32[256,128]{1,0:T(8,128)} %constant.4.clone.cosr, f32[256,128]{1,0:T(8,128)} %constant.5.clone.sinr, f32[1,1024]{1,0:T(1,128)} %bitcast.7, ...), custom_call_target="tpu_custom_call" | custom-call | tf_op jit(solution)/shard_map/layer/pallas_call | solution.py:716
  127.2 1.4 %copy.19 = f32[16,8]{0,1:T(8,128)} copy(f32[16,8]{1,0:T(8,128)} %layer.1) | data formatting | bytes 1024 | tf_op jit(solution)/shard_map/layer/pallas_call | solution.py:716

commit v6 on v5

--- a/solution.py
+++ b/solution.py
@@ -128,13 +128,32 @@
 
 
 class FlowDeep(Flow):
-    def start0(self):
+    def start_x(self):
         p = self.pos
         pltpu.make_async_remote_copy(
             src_ref=self.own, dst_ref=self.block(p.d), send_sem=self.ss(X0), recv_sem=self.rs(X0),
             device_id={"dp": p.xpeer, "tensor": p.xsib}, device_id_type=MESH).start()
-        for kind, dev in ((R1, p.up), (L1, p.down), (C0, p.cpeer)):
-            self.copy(kind, p.d, dev, own=True).start()
+        self.copy(C0, p.d, p.cpeer, own=True).start()
+
+    def start_y(self):
+        p = self.pos
+        self.copy(R1, p.d, p.up, own=True).start()
+        self.copy(L1, p.d, p.down, own=True).start()
+
+    def pass_x(self):
+        p = self.pos
+        self.got(X0)
+        self.forward(R2, p.xpeer, p.up)
+        self.forward(L2, p.xpeer, p.down)
+        self.to_core(X0)
+
+    def stage1(self):
+        p = self.pos
+        self.got(R1)
+        self.forward(R3, p.down, p.up)
+        self.to_core(R1)
+        self.got(L1)
+        self.to_core(L1)
 
 
 class FlowY(Flow):
@@ -376,6 +395,7 @@
     erings[0].step(2)
     flow(1).stage2()
     flow(2).stage2()
+    deep.start_x()
     mixer.stage1()
     erings[1].step(2)
     project((2, 4))
@@ -383,7 +403,7 @@
         flow(f).stage3()
     mixer.stage2()
     loads[7].wait()
-    deep.start0()
+    deep.start_y()
     din_part = pl.ds(pl.multiple_of(128 * p.core, 128), 128)
     din_rest = pl.ds(pl.multiple_of(128 - 128 * p.core, 128), 128)
     din_x = pltpu.make_async_remote_copy(
@@ -424,6 +444,7 @@
         return carry
 
     lax.fori_loop(0, 2, attend, 0, unroll=2)
+    deep.pass_x()
     erings[1].step(3)
     mixer.stage3()
     mixer.stage4()
@@ -462,6 +483,7 @@
     lax.fori_loop(1, 3, crossed, 0)
     for n in range(2):
         prings[n].step(1)
+    deep.stage1()
     din_x.wait_recv()
     din_core(din_part).start()
     lax.fori_loop(3, 5, crossed, 0)
@@ -476,7 +498,7 @@
     lax.fori_loop(5, 7, crossed, 0)
     for n in range(2):
         prings[n].step(3)
-    deep.stage1()
+    deep.stage2()
     for n in range(2):
         erings[n].arrive()
         mine = pl.ds(4 * n, 4)
@@ -499,7 +521,6 @@
         src_ref=heads.at[head_part], dst_ref=hx.at[head_part], send_sem=hss.at[0],
         recv_sem=hrs.at[0], device_id={"tensor": p.xsib}, device_id_type=MESH)
     head_x.start()
-    deep.stage2()
     loads[6].wait()
     din_core(din_rest).wait_recv()
 
@@ -569,24 +590,23 @@
 
     lax.fori_loop(0, 3, dproject, 0, unroll=3)
 
-    rq = lax.broadcasted_iota(jnp.int32, (rows, rows), 0)
-    rk = lax.broadcasted_iota(jnp.int32, (rows, rows), 1)
+    rq = lax.rem(lax.broadcasted_iota(jnp.int32, (2 * rows, rows), 0), rows)
+    rk = lax.broadcasted_iota(jnp.int32, (2 * rows, rows), 1)
     seen = (lax.rem(rq, OWN) == lax.rem(rk, OWN)) & (rq >= rk)
     low_half = lax.broadcasted_iota(jnp.int32, (rows, 128), 1) < DHEAD_DIM
 
     def dattend(j, carry):
         cols = pl.ds(pl.multiple_of(j * 128, 128), 128)
         q, k, v = proj[0, :, cols], proj[1, :, cols], proj[2, :, cols]
-        parts = []
-        for half in (low_half, jnp.logical_not(low_half)):
-            scores = dot_t(jnp.where(half, q, jnp.zeros_like(q)), k) * DHEAD_DIM ** (-0.5)
-            e = jnp.where(seen, jnp.exp(jnp.where(seen, scores, 0.0)), 0.0)
-            w = (e / jnp.sum(e, axis=-1, keepdims=True)).astype(BF16)
-            parts.append(dot(w, v))
-        datt[:, cols] = jnp.where(low_half, parts[0], parts[1]).astype(BF16)
-        return carry
-
-    lax.fori_loop(0, DHEADS // 2, dattend, 0, unroll=4)
+        both = jnp.concatenate([jnp.where(low_half, q, jnp.zeros_like(q)), jnp.where(low_half, jnp.zeros_like(q), q)], axis=0)
+        scores = dot_t(both, k) * DHEAD_DIM ** (-0.5)
+        e = jnp.where(seen, jnp.exp(jnp.where(seen, scores, 0.0)), 0.0)
+        w = (e / jnp.sum(e, axis=-1, keepdims=True)).astype(BF16)
+        outs = dot(w, v)
+        datt[:, cols] = jnp.where(low_half, outs[:rows], outs[rows:]).astype(BF16)
+        return carry
+
+    lax.fori_loop(0, DHEADS // 2, dattend, 0, unroll=8)
     loads[8].wait()
     out = x + dot(datt[...], wm[...])
     final = (out * lax.rsqrt(jnp.mean(out * out, axis=-1, keepdims=True) + epsilon) * fgain[...]).astype(BF16)

time: 129 us -> 120 us (0.930)
  Pallas kernels: 126 us -> 117 us
    pallas_call x1, Pallas kernels: 126 us -> 117 us  [shards(): pl.pallas_call(layer, out_shape=jax.ShapeDtypeStruct((OWN, CODEBOOKS), F3...]
where the time goes in v6:
time: 120 us
  Pallas kernels  117 us (98%)
  local copies, waits for them, and re-layouts  2.82 us (2%)
    pallas_call x1, Pallas kernels, shards(): pl.pallas_call(layer, out_shape=jax.ShapeDtypeStruct((OWN, CODEBOOKS), F3...  117 us

profile of v6, /device:TPU:4, one launch (start us, length us, event | category | flops | bytes accessed | tf_op | source)
XLA Modules:
  0.0 119.8 jit_solution(15090372662108605071)
XLA Ops:
  0.0 1.5 %copy.18.code = s32[256,8]{1,0:T(8,128)} copy(s32[256,8]{0,1:T(8,128)} %param.31) | data formatting | bytes 16384 | tf_op args[14]
  1.5 116.9 %layer.1 = f32[16,8]{1,0:T(8,128)} custom-call(f32[1,4096]{1,0:T(1,128)} %bitcast.5, f32[1,4096]{1,0:T(1,128)} %bitcast.6, s32[2,128]{1,0:T(2,128)} %bitcast.9, s32[256,8]{1,0:T(8,128)} %copy.18.code, f32[256,128]{1,0:T(8,128)} %constant.4.clone.cosr, f32[256,128]{1,0:T(8,128)} %constant.5.clone.sinr, f32[1,1024]{1,0:T(1,128)} %bitcast.7, ...), custom_call_target="tpu_custom_call" | custom-call | tf_op jit(solution)/shard_map/layer/pallas_call | solution.py:736
  118.4 1.4 %copy.19 = f32[16,8]{0,1:T(8,128)} copy(f32[16,8]{1,0:T(8,128)} %layer.1) | data formatting | bytes 1024 | tf_op jit(solution)/shard_map/layer/pallas_call | solution.py:736

commit v7 on v6

--- a/solution.py
+++ b/solution.py
@@ -247,10 +247,10 @@
                 self.copy(way, s).wait_send()
 
 
-def layer(gain, ogain, tid, code, cosr, sinr, dgain, fgain,
+def layer(gain, ogain, tid, code_t, cosr, sinr, dgain, fgain,
           hid_h, text_h, qkv_h, mix_h, din_h, tabs_h, dqkv, dmix_h, heads,
           loss,
-          hid, text, hown, din, tabs, goal, wall, normed, acc, att, part, emb, er, el, eo, ei, pr, pe, po, pi, bs, br,
+          hid, text, hown, din, tabs, goal, code, wall, normed, acc, att, part, emb, er, el, eo, ei, pr, pe, po, pi, bs, br,
           cs, cr, xin, wq, wm, wh, hx, proj, datt, fin, sums, got,
           lsem, wss, wrs, ess, ers, pss, prs, bss, brs, xss, xrs, css, crs, hss, hrs, fss, frs, tss, trs):
     p = Places()
@@ -320,7 +320,8 @@
     for f in range(3):
         flow(f).start0()
 
-    codev = code[...].astype(F32)
+    codev = code_t[...].astype(F32).T
+    code[...] = codev
     pick = lax.broadcasted_iota(jnp.int32, codev.shape, 1)
     count = text.shape[0]
     whole = count // 128 * 128
@@ -444,9 +445,9 @@
         return carry
 
     lax.fori_loop(0, 2, attend, 0, unroll=2)
-    deep.pass_x()
     erings[1].step(3)
     mixer.stage3()
+    deep.pass_x()
     mixer.stage4()
 
     def cross(zz):
@@ -667,7 +668,7 @@
     shared = OWN * NZ
     lanes = lax.broadcasted_iota(jnp.int32, (shared, 256), 1).astype(F32)
     spots = lax.broadcasted_iota(jnp.int32, (shared, 128), 1)
-    goals = goal[...].astype(F32) - (z * 256).astype(F32)
+    goals = goal[...] - (z * 256).astype(F32)
     books = lax.broadcasted_iota(jnp.int32, goals.shape, 1)
 
     def book(c, total):
@@ -740,7 +741,7 @@
         out_specs=vmem,
         scratch_shapes=[
             b16(FRAMES, D), b16(*text_table.shape), b16(128, 512), b16(2, 256, DD), b16(CODEBOOKS - 1, 128, DD),
-            pltpu.VMEM((128, CODEBOOKS), jnp.int32),
+            f32(128, CODEBOOKS), f32(FRAMES, CODEBOOKS),
             b16(4, DP, 256, 256), b16(FRAMES, D), f32(3, FRAMES, 256), b16(FRAMES, 256),
             b16(NZ, 3, 128, 256),
             b16(TP, CODEBOOKS, OWN, DD),
@@ -766,7 +767,7 @@
         compiler_params=pltpu.CompilerParams(
             collective_id=0, has_side_effects=True, vmem_limit_bytes=60 * 2**20),
         name="layer",
-    )(attn_gain[None], out_gain[None], text_ids.reshape(2, 128), codes, cosv, sinv, depth_gain[None],
+    )(attn_gain[None], out_gain[None], text_ids.reshape(2, 128), codes.T, cosv, sinv, depth_gain[None],
       final_gain[None],
       hidden_in, text_table, qkv_weight, mix_weight, depth_in_weight, code_tables, depth_qkv, depth_mix, heads_weight)
 

time: 120 us -> 119 us (level)
  local copies, waits for them, and re-layouts: 2.82 us -> 1.36 us
    unnamed x1 -> x0, local copies, waits for them, and re-layouts: 1.47 us -> none
where the time goes in v7:
time: 119 us; the launch traced here: 118 us
  Pallas kernels  117 us (98%)
  local copies, waits for them, and re-layouts  1.36 us (1%)
    pallas_call x1, Pallas kernels, shards(): pl.pallas_call(layer, out_shape=jax.ShapeDtypeStruct((OWN, CODEBOOKS), F3...  117 us

profile of v7, /device:TPU:4, one launch (start us, length us, event | category | flops | bytes accessed | tf_op | source)
XLA Modules:
  0.0 118.0 jit_solution(15464396870010974373)
XLA Ops:
  0.0 116.7 %layer.1 = f32[16,8]{1,0:T(8,128)} custom-call(f32[1,4096]{1,0:T(1,128)} %bitcast.6, f32[1,4096]{1,0:T(1,128)} %bitcast.7, s32[2,128]{1,0:T(2,128)} %bitcast.11, s32[8,256]{1,0:T(8,128)} %bitcast.8, f32[256,128]{1,0:T(8,128)} %constant.4.clone.cosr, f32[256,128]{1,0:T(8,128)} %constant.5.clone.sinr, f32[1,1024]{1,0:T(1,128)} %bitcast.9, f32[1,1024]{1,0:T(1,128)} %bitcast.10, ...), custom_call_target="tpu_custom_call" | custom-call | tf_op jit(solution)/shard_map/layer/pallas_call | solution.py:737
  116.7 1.4 %copy.18 = f32[16,8]{0,1:T(8,128)} copy(f32[16,8]{1,0:T(8,128)} %layer.1) | data formatting | bytes 1024 | tf_op jit(solution)/shard_map/layer/pallas_call | solution.py:737

commit v8 on v7

--- a/solution.py
+++ b/solution.py
@@ -481,13 +481,13 @@
     crossed(0, 0)
     for n in range(2):
         prings[n].step(0)
-    lax.fori_loop(1, 3, crossed, 0)
+    lax.fori_loop(1, 3, crossed, 0, unroll=2)
     for n in range(2):
         prings[n].step(1)
     deep.stage1()
     din_x.wait_recv()
     din_core(din_part).start()
-    lax.fori_loop(3, 5, crossed, 0)
+    lax.fori_loop(3, 5, crossed, 0, unroll=2)
     for n in range(2):
         prings[n].step(2)
 
@@ -496,7 +496,7 @@
             src_ref=src, dst_ref=dst, send_sem=xss.at[k], recv_sem=xrs.at[k],
             device_id={"tensor": p.xsib}, device_id_type=MESH)
 
-    lax.fori_loop(5, 7, crossed, 0)
+    lax.fori_loop(5, 7, crossed, 0, unroll=2)
     for n in range(2):
         prings[n].step(3)
     deep.stage2()
@@ -571,7 +571,7 @@
         hl = v[:, DD:].astype(F32)
         return context + v[:, :DD].astype(F32), square + hl[:, :1] + hl[:, 64:65]
 
-    context, square = lax.fori_loop(0, NZ, gathered, (jnp.zeros((OWN, DD), F32), jnp.zeros((OWN, 1), F32)))
+    context, square = lax.fori_loop(0, NZ, gathered, (jnp.zeros((OWN, DD), F32), jnp.zeros((OWN, 1), F32)), unroll=8)
     context = context * lax.rsqrt(square / D + epsilon)
 
     def ring(n, way, s, block):

time: 119 us -> 119 us (level)
  no operation moved by 1% of the time
where the time goes in v8:
time: 119 us; the launch traced here: 118 us
  Pallas kernels  116 us (97%)
  local copies, waits for them, and re-layouts  1.36 us (1%)
    pallas_call x1, Pallas kernels, shards(): pl.pallas_call(layer, out_shape=jax.ShapeDtypeStruct((OWN, CODEBOOKS), F3...  116 us

profile of v8, /device:TPU:4, one launch (start us, length us, event | category | flops | bytes accessed | tf_op | source)
XLA Modules:
  0.0 117.8 jit_solution(16341853267542500459)
XLA Ops:
  0.0 116.4 %layer.1 = f32[16,8]{1,0:T(8,128)} custom-call(f32[1,4096]{1,0:T(1,128)} %bitcast.6, f32[1,4096]{1,0:T(1,128)} %bitcast.7, s32[2,128]{1,0:T(2,128)} %bitcast.11, s32[8,256]{1,0:T(8,128)} %bitcast.8, f32[256,128]{1,0:T(8,128)} %constant.4.clone.cosr, f32[256,128]{1,0:T(8,128)} %constant.5.clone.sinr, f32[1,1024]{1,0:T(1,128)} %bitcast.9, f32[1,1024]{1,0:T(1,128)} %bitcast.10, ...), custom_call_target="tpu_custom_call" | custom-call | tf_op jit(solution)/shard_map/layer/pallas_call | solution.py:737
  116.4 1.4 %copy.18 = f32[16,8]{0,1:T(8,128)} copy(f32[16,8]{1,0:T(8,128)} %layer.1) | data formatting | bytes 1024 | tf_op jit(solution)/shard_map/layer/pallas_call | solution.py:737
